TPU v7x, 32 devices: a whole 2x2x4 slice. The times are simulated.
32 devices in a mesh: ctx: 8 (over z, y), ch: 4 (over x, core).
Axes of the slice: x: 2, y: 2, z: 4, core: 2. Of those that a mesh axis runs over, the one named last changes fastest.
Arguments:
- q_li: bfloat16 [4096, 8192], P('ctx', 'ch'), may hold values from -6 to 6
- k_li: bfloat16 [4096, 8192], P('ctx', 'ch'), may hold values from -6 to 6
- v_li: bfloat16 [4096, 8192], P('ctx', 'ch'), may hold values from -6 to 6
- q_att: bfloat16 [4096, 8192], P('ctx', 'ch'), may hold values from -5 to 5
- k_att: bfloat16 [4096, 8192], P('ctx', 'ch'), may hold values from -5 to 5
- cotangent: bfloat16 [4096, 8192], P('ctx', 'ch'), may hold values from -6 to 6
- record_ids: int32 [4096], P('ctx'), may hold values from 0 to 7, never falling along the last dimension, each value on 1 to 1024 neighbouring positions
- decay_rate: float32 [16, 8192], P(None, 'ch'), may hold values from 2.4414062e-06 to 0.04
- residue: float32 [16, 8192], P(None, 'ch'), may hold values from -6 to 6
- norm_gain: float32 [8192], P('ch'), may hold values from 0.1 to 1.9
Outputs:
- attended: bfloat16 [4096, 8192], P('ctx', 'ch')
- d_q_att: bfloat16 [4096, 8192], P('ctx', 'ch')
- d_k_att: bfloat16 [4096, 8192], P('ctx', 'ch')
- d_q_li: bfloat16 [4096, 8192], P('ctx', 'ch')
- d_k_li: bfloat16 [4096, 8192], P('ctx', 'ch')
- d_v_li: bfloat16 [4096, 8192], P('ctx', 'ch')
Inputs may be any that keep to these rules, and one draw needn't show every extreme that they name: `record_ids`: record numbers never fall along the sequence; every record holds 1 to 1024 positions, and some record holds exactly 1024.
All inputs are finite; a program needn't handle non-finite values.
Results may differ from a plain program's by a relative error of at most 0.017.
Values may be sent and summed in bfloat16 or wider, within the bound.
A program may use at most 320 MiB of HBM per device.

v0:
```python
import math

import jax
import jax.numpy as jnp
from jax import lax
from jax.sharding import PartitionSpec as P

D = 8192
HEAD_DIM = 128
SPAN = 2


EPS = 1e-06
HIGH = lax.Precision.HIGHEST
NEG = -1e30


def shifted(value, axis, steps):
    count = lax.axis_size(axis)
    initial, last = (max(0, -steps), min(count, count - steps))
    return lax.ppermute(value, axis, [(source, source + steps) for source in range(initial, last)])


def channel_total(partial_value):
    return lax.psum(partial_value, "ch")


def carried_state(slab_rate, local_state, backward):
    slab_count = lax.axis_size("ctx")
    collected = lax.all_gather(local_state[None], "ctx", axis=0, tiled=True)
    position = lax.axis_index("ctx")
    others = jnp.arange(slab_count, dtype=jnp.int32)
    if backward:
        spacing = others - position - 1
    else:
        spacing = position - 1 - others
    distances = jnp.maximum(spacing, 0).astype(jnp.float32)
    weights = jnp.where(
        spacing[:, None, None] >= 0, jnp.exp(-slab_rate[None] * distances[:, None, None]), 0.0
    )
    return jnp.sum(weights * collected, axis=0)


def filter_pieces(decay_rate, residue, block):
    inject = jnp.sqrt(-jnp.expm1(-2.0 * decay_rate))
    offsets = jnp.arange(block, dtype=jnp.float32)
    ramping = jnp.exp(-decay_rate[:, None, :] * offsets[None, :, None])
    filter_taps = jnp.sum((residue * inject)[:, None, :] * ramping, axis=0)
    differ = offsets[:, None] - offsets[None, :]
    selector = (differ[:, :, None] == offsets[None, None, :]).astype(jnp.float32)
    toeplitz = jnp.dot(selector.reshape(block * block, block), filter_taps, precision=HIGH).reshape(
        block, block, filter_taps.shape[1]
    )
    toeplitz_high = toeplitz.astype(jnp.bfloat16)
    toeplitz_rest = (toeplitz - toeplitz_high.astype(jnp.float32)).astype(jnp.bfloat16)
    return (inject, ramping, (toeplitz_high, toeplitz_rest))


def mix_forward(signal, decay_rate, residue, block):
    inject, ramping, toeplitz = filter_pieces(decay_rate, residue, block)
    block_count = signal.shape[0] // block
    blocks = signal.reshape(block_count, block, signal.shape[1])
    block_decay = jnp.exp(-decay_rate * block)
    tail_weight = inject[:, None, :] * ramping[:, ::-1, :]
    block_ends = jnp.einsum("nqc,bqc->bnc", tail_weight, blocks.astype(jnp.float32), precision=HIGH)

    def advance(carry_state, block_end):
        return (block_decay * carry_state + block_end, carry_state)

    local_end, entering = lax.scan(advance, jnp.zeros_like(block_decay), block_ends)
    lead_weight = residue[:, None, :] * ramping * jnp.exp(-decay_rate)[:, None, :]
    inside = jnp.einsum("tsc,bsc->btc", toeplitz[0], blocks, preferred_element_type=jnp.float32)
    inside = inside + jnp.einsum(
        "tsc,bsc->btc", toeplitz[1], blocks, preferred_element_type=jnp.float32
    )
    return (local_end, (entering, lead_weight, inside))


def mix_finish(pieces, incoming, decay_rate, block):
    entering, lead_weight, inside = pieces
    block_count = entering.shape[0]
    distances = jnp.arange(block_count, dtype=jnp.float32) * block
    entering = entering + jnp.exp(-decay_rate[None] * distances[:, None, None]) * incoming[None]
    across = jnp.einsum("nqc,bnc->bqc", lead_weight, entering, precision=HIGH)
    return (inside + across).reshape(block_count * block, inside.shape[2])


def mix_backward(gradient, decay_rate, residue, block):
    inject, ramping, toeplitz = filter_pieces(decay_rate, residue, block)
    block_count = gradient.shape[0] // block
    blocks = gradient.reshape(block_count, block, gradient.shape[1])
    block_decay = jnp.exp(-decay_rate * block)
    start_weight = residue[:, None, :] * ramping
    block_starts = jnp.einsum(
        "nqc,bqc->bnc", start_weight, blocks.astype(jnp.float32), precision=HIGH
    )

    def retreat(carry_state, block_start):
        return (block_decay * carry_state + block_start, carry_state)

    local_start, arriving = lax.scan(
        retreat, jnp.zeros_like(block_decay), block_starts, reverse=True
    )
    back_weight = inject[:, None, :] * ramping[:, ::-1, :] * jnp.exp(-decay_rate)[:, None, :]
    inside = jnp.einsum("tsc,btc->bsc", toeplitz[0], blocks, preferred_element_type=jnp.float32)
    inside = inside + jnp.einsum(
        "tsc,btc->bsc", toeplitz[1], blocks, preferred_element_type=jnp.float32
    )
    return (local_start, (arriving, back_weight, inside))


def mix_back_finish(pieces, incoming, decay_rate, block):
    arriving, back_weight, inside = pieces
    block_count = arriving.shape[0]
    distances = (block_count - 1 - jnp.arange(block_count, dtype=jnp.float32)) * block
    arriving = arriving + jnp.exp(-decay_rate[None] * distances[:, None, None]) * incoming[None]
    across = jnp.einsum("nqc,bnc->bqc", back_weight, arriving, precision=HIGH)
    return (inside + across).reshape(block_count * block, inside.shape[2])


def head_columns(array, head_index):
    return lax.dynamic_slice_in_dim(array, head_index * HEAD_DIM, HEAD_DIM, 1)


def pair_products(left_rows, right_rows):
    return lax.dot_general(
        left_rows, right_rows, (((1,), (1,)), ((), ())), preferred_element_type=jnp.float32
    )


def column_products(left_rows, right_rows):
    return lax.dot_general(
        left_rows, right_rows, (((0,), (0,)), ((), ())), preferred_element_type=jnp.float32
    )


def masked_scores(queries, key_rows, allowed, score_scale):
    return jnp.where(allowed, pair_products(queries, key_rows) * score_scale, NEG)


def merge_heads(array):
    return jnp.transpose(array, (1, 0, 2)).reshape(array.shape[1], array.shape[0] * array.shape[2])


def rounded(array):
    return lax.optimization_barrier(array.astype(jnp.bfloat16)).astype(jnp.float32)


def local(q_li, k_li, v_li, q_att, k_att, cotangent, record_ids, decay_rate, residue, norm_gain):
    tokens, channels = q_li.shape
    block = math.gcd(tokens, 64)
    head_count = channels // HEAD_DIM
    score_scale = HEAD_DIM ** (-0.5)
    slab_rate = decay_rate * tokens
    record_marks = (record_ids + 1).astype(jnp.bfloat16)
    key_list = [k_att]
    mark_list = [record_marks]
    mixed_input = (k_li.astype(jnp.float32) * v_li.astype(jnp.float32)).astype(jnp.bfloat16)
    local_end, forward_pieces = mix_forward(mixed_input, decay_rate, residue, block)
    incoming = carried_state(slab_rate, local_end, False)
    mixed = mix_finish(forward_pieces, incoming, decay_rate, block)
    lifted = q_li.astype(jnp.float32) * mixed
    inv_rms = lax.rsqrt(channel_total(jnp.sum(lifted * lifted, axis=1)) / D + EPS)
    values = (lifted * inv_rms[:, None] * norm_gain[None, :]).astype(jnp.bfloat16)
    value_list = [values]
    for distance in range(1, SPAN + 1):
        far_keys, far_values, far_marks = shifted((k_att, values, record_marks), "ctx", distance)
        key_list.append(far_keys)
        value_list.append(far_values)
        mark_list.append(far_marks)
    keys_all = jnp.concatenate(key_list, axis=0)
    values_all = jnp.concatenate(value_list, axis=0)
    marks_all = jnp.concatenate(mark_list, axis=0)
    row_index = jnp.arange(tokens, dtype=jnp.int32)
    column_index = jnp.arange(keys_all.shape[0], dtype=jnp.int32)
    allowed = (record_marks[:, None] == marks_all[None, :]) & (
        (column_index[None, :] >= tokens) | (column_index[None, :] <= row_index[:, None])
    )
    head_numbers = jnp.arange(head_count, dtype=jnp.int32)

    def forward_head(head_index):
        queries = head_columns(q_att, head_index)
        scores = masked_scores(queries, head_columns(keys_all, head_index), allowed, score_scale)
        row_top = jnp.max(scores, axis=1)
        exponent = jnp.exp(scores - row_top[:, None])
        row_total = jnp.sum(exponent, axis=1)
        weights_low = (exponent / row_total[:, None]).astype(jnp.bfloat16)
        output = jnp.dot(
            weights_low, head_columns(values_all, head_index), preferred_element_type=jnp.float32
        )
        row_delta = jnp.sum(
            head_columns(cotangent, head_index).astype(jnp.float32) * output, axis=1
        )
        return (output.astype(jnp.bfloat16), row_top, row_total, row_delta)

    head_outputs, row_tops, row_totals, row_deltas = lax.map(forward_head, head_numbers)
    attended = merge_heads(head_outputs)
    key_span = keys_all.shape[0]

    def backward_head(pieces):
        head_index, row_top, row_total, row_delta = pieces
        queries = head_columns(q_att, head_index)
        key_rows = head_columns(keys_all, head_index)
        grads_out = head_columns(cotangent, head_index)
        scores = masked_scores(queries, key_rows, allowed, score_scale)
        probs = jnp.exp(scores - row_top[:, None]) / row_total[:, None]
        prob_grad = pair_products(grads_out, head_columns(values_all, head_index))
        dscore = (probs * (prob_grad - row_delta[:, None])).astype(jnp.bfloat16)
        query_grad = jnp.dot(dscore, key_rows, preferred_element_type=jnp.float32) * score_scale
        key_grad = column_products(dscore, queries) * score_scale
        value_grad = column_products(probs.astype(jnp.bfloat16), grads_out)
        return (query_grad.astype(jnp.bfloat16), key_grad, value_grad)

    query_grads, key_grads, value_grads = lax.map(
        backward_head, (head_numbers, row_tops, row_totals, row_deltas)
    )
    d_q_att = merge_heads(query_grads)
    key_merged = merge_heads(key_grads)
    value_merged = merge_heads(value_grads)
    key_total = rounded(key_merged[:tokens])
    value_total = rounded(value_merged[:tokens])
    for distance in range(1, SPAN + 1):
        lower = distance * tokens
        back_keys, back_values = shifted(
            (
                key_merged[lower : lower + tokens].astype(jnp.bfloat16),
                value_merged[lower : lower + tokens].astype(jnp.bfloat16),
            ),
            "ctx",
            -distance,
        )
        key_total = key_total + back_keys.astype(jnp.float32)
        value_total = value_total + back_values.astype(jnp.float32)
    d_k_att = key_total.astype(jnp.bfloat16)
    weighted = value_total * norm_gain[None, :]
    inner = channel_total(jnp.sum(lifted * weighted, axis=1))
    lifted_grad = inv_rms[:, None] * weighted - lifted * (inv_rms**3)[:, None] * inner[:, None] / D
    d_q_li = (lifted_grad * mixed).astype(jnp.bfloat16)
    mixed_grad = (lifted_grad * q_li.astype(jnp.float32)).astype(jnp.bfloat16)
    local_start, backward_pieces = mix_backward(mixed_grad, decay_rate, residue, block)
    arriving = carried_state(slab_rate, local_start, True)
    input_grad = mix_back_finish(backward_pieces, arriving, decay_rate, block)
    d_k_li = (input_grad * v_li.astype(jnp.float32)).astype(jnp.bfloat16)
    d_v_li = (input_grad * k_li.astype(jnp.float32)).astype(jnp.bfloat16)
    return (attended, d_q_att, d_k_att, d_q_li, d_k_li, d_v_li)


def solution(mesh):
    placed = (
        P("ctx", "ch"),
        P("ctx", "ch"),
        P("ctx", "ch"),
        P("ctx", "ch"),
        P("ctx", "ch"),
        P("ctx", "ch"),
        P("ctx"),
        P(None, "ch"),
        P(None, "ch"),
        P("ch"),
    )
    return jax.shard_map(
        local,
        mesh=mesh,
        in_specs=placed,
        out_specs=(
            P("ctx", "ch"),
            P("ctx", "ch"),
            P("ctx", "ch"),
            P("ctx", "ch"),
            P("ctx", "ch"),
            P("ctx", "ch"),
        ),
        check_vma=False,
    )
```

profile of v0, /device:TPU:8, one launch (start us, length us, event | category | flops | bytes accessed | tf_op | source)
XLA Modules:
  0.0 1018.3 jit_solution(4700522389123663766)
XLA Ops:
  23.0 12.8 %multiply_exponential_fusion = (f32[16,64,2048]{1,0,2:T(8,128)}, f32[64,2048]{0,1:T(8,128)S(1)}) fusion(f32[16,2048]{0,1:T(8,128)S(1)} %copy.81, f32[16,2048]{0,1:T(8,128)S(1)} %copy.80), kind=kLoop, calls=%fused_computation.65 | loop fusion | flops 6160384 | bytes 9175040 | tf_op jit(solution)/shard_map/exp | solution.py:47
  35.8 24.9 %rev.4 = f32[16,64,2048]{1,0,2:T(8,128)} reverse(f32[16,64,2048]{1,0,2:T(8,128)} %get-tuple-element.543), dimensions={1} | reverse | bytes 16777216 | tf_op jit(solution)/shard_map/rev | solution.py:64
  61.9 19.5 %fusion.68 = f32[8,16,2048]{1,0,2:T(8,128)} fusion(bf16[8,64,2048]{1,0,2:T(8,128)(2,1)} %copy.83, f32[16,64,2048]{1,0,2:T(8,128)} %rev.4, f32[16,2048]{0,1:T(8,128)S(1)} %copy.87), kind=kOutput, calls=%fused_computation.102 | convolution fusion | flops 203423744 | bytes 11665408 | tf_op jit(solution)/shard_map/nqc,bqc->bnc/dot_general | solution.py:65
  81.4 6.0 copy.89
  87.5 8.2 while.64
  99.0 18.0 %subtract_convert_fusion = (bf16[64,64,2048]{2,1,0:T(8,128)(2,1)}, bf16[64,64,2048]{2,1,0:T(8,128)(2,1)}) fusion(f32[64,2048]{0,1:T(8,128)S(1)} %get-tuple-element.544, f32[64,64]{1,0:T(8,128)S(1)} %iota_subtract_fusion), kind=kOutput, calls=%fused_computation.59 | convolution fusion | flops 6476267520 | bytes 34095104 | tf_op jit(solution)/shard_map/dot_general | solution.py:51
  117.0 46.0 %copy.84 = bf16[64,64,2048]{1,0,2:T(8,128)(2,1)} copy(bf16[64,64,2048]{2,1,0:T(8,128)(2,1)} %get-tuple-element.526) | data formatting | bytes 33554432 | tf_op jit(solution)/shard_map/convert_element_type | solution.py:54
  163.0 23.9 %fusion.81 = f32[2048,8,64]{2,1,0:T(8,128)} fusion(bf16[8,64,2048]{1,0,2:T(8,128)(2,1)} %copy.83, bf16[64,64,2048]{1,0,2:T(8,128)(2,1)} %copy.84), kind=kOutput, calls=%fused_computation.148 | convolution fusion | flops 134217728 | bytes 23068672 | tf_op jit(solution)/shard_map/tsc,bsc->btc/dot_general | solution.py:72
  186.9 46.0 %copy.86 = bf16[64,64,2048]{1,0,2:T(8,128)(2,1)} copy(bf16[64,64,2048]{2,1,0:T(8,128)(2,1)} %get-tuple-element.525) | data formatting | bytes 33554432 | tf_op jit(solution)/shard_map/convert_element_type | solution.py:55
  233.2 24.3 %fusion.82 = f32[2048,8,64]{2,1,0:T(8,128)} fusion(bf16[8,64,2048]{1,0,2:T(8,128)(2,1)} %copy.83, bf16[64,64,2048]{1,0,2:T(8,128)(2,1)} %copy.86), kind=kOutput, calls=%fused_computation.149 | convolution fusion | flops 134217728 | bytes 23068672 | tf_op jit(solution)/shard_map/tsc,bsc->btc/dot_general | solution.py:73
  265.1 29.7 %add_bitcast_fusion.1 = f32[8,64,2048]{1,0,2:T(8,128)} fusion(f32[2048,8,64]{2,1,0:T(8,128)} %fusion.81, f32[2048,8,64]{2,1,0:T(8,128)} %fusion.82, f32[8,16,2048]{1,0,2:T(8,128)} %copy.92, f32[16,2048]{0,1:T(8,128)S(1)} %copy.91, f32[16,2048]{0,1:T(8,128)} %copy.90, f32[16,2048]{0,1:T(8,128)S(1)} %copy.81), kind=kOutput, calls=%fused_computation.73 | convolution fusion | flops 209715200 | bytes 14024704 | tf_op jit(solution)/shard_map/nqc,bnc->bqc/dot_general | solution.py:84
  294.8 7.2 copy.93
  304.8 6.0 psum.14
  324.3 40.1 %collective-permute-done.3 = bf16[512]{0:T(512)(128)(2,1)S(1)} collective-permute-done((bf16[512]{0:T(512)(128)(2,1)S(1)}, bf16[512]{0:T(512)(128)(2,1)S(1)}, u32[]{:S(2)}, u32[]{:S(2)}) %collective-permute-start.3) | collective-permute-done | bytes 1056 | tf_op jit(solution)/shard_map/ppermute | solution.py:21
  364.4 48.3 %collective-permute-start.2 = (bf16[512]{0:T(512)(128)(2,1)S(1)}, bf16[512]{0:T(512)(128)(2,1)S(1)}, u32[]{:S(2)}, u32[]{:S(2)}) collective-permute-start(bf16[512]{0:T(512)(128)(2,1)S(1)} %add_convert_fusion.1), channel_id=1, source_target_pairs={{0,4},{4,8},{8,12},{12,16},{16,20},{20,24},{24,28},{1,5},{5,9},{9,... | collective-permute-start | bytes 3080 | tf_op jit(solution)/shard_map/ppermute | solution.py:21
  420.3 6.1 pad_maximum_fusion
  426.4 123.4 %while.62 = (s32[]{:T(128)}, bf16[16,512,128]{1,2,0:T(8,128)(2,1)}, f32[16,512]{1,0:T(8,128)S(1)}, f32[16,512]{1,0:T(8,128)S(1)}, f32[16,512]{1,0:T(8,128)S(1)},...) while((s32[]{:T(128)}, bf16[16,512,128]{1,2,0:T(8,128)(2,1)}, ...), condition=%wide.region_10.11_spmd.clone, body=%wide.region_6.10_spmd.clone.sunk | while | flops 413923840 | bytes 11696887 | solution.py:196
  549.8 193.5 %while.63 = (s32[]{:T(128)}, bf16[16,512,128]{2,1,0:T(8,128)(2,1)}, bf16[16,1536,128]{2,1,0:T(8,128)(2,1)}, bf16[16,1536,128]{2,1,0:T(8,128)(2,1)}, s32[16]{0:T(...) while((s32[]{:T(128)}, bf16[16,512,128]{2,1,0:T(8,128)(2,1)}, ...), condition=%wide.region_12.13_spmd.clone, body=%wide.region_11.12_spmd.clone.sunk | while | flops 1017970688 | bytes 17590032 | solution.py:214
  743.3 4.9 slice_bitcast_fusion.2
  776.0 24.9 %collective-permute-done.9 = bf16[512,2048]{1,0:T(8,128)(2,1)} collective-permute-done((bf16[512,2048]{1,0:T(8,128)(2,1)}, bf16[512,2048]{1,0:T(8,128)(2,1)}, u32[]{:S(2)}, u32[]{:S(2)}) %collective-permute-start.9) | collective-permute-done | bytes 2097184 | tf_op jit(solution)/shard_map/ppermute | solution.py:21
  800.9 42.5 %collective-permute-done.8 = bf16[512,2048]{1,0:T(8,128)(2,1)} collective-permute-done((bf16[512,2048]{1,0:T(8,128)(2,1)}, bf16[512,2048]{1,0:T(8,128)(2,1)}, u32[]{:S(2)}, u32[]{:S(2)}) %collective-permute-start.8) | collective-permute-done | bytes 2097184 | tf_op jit(solution)/shard_map/ppermute | solution.py:21
  847.0 6.3 psum.15
  853.3 6.9 fusion.59
  860.3 5.8 copy.104
  866.1 21.8 %fusion.71 = f32[8,16,2048]{1,0,2:T(8,128)} fusion(bf16[8,64,2048]{1,0,2:T(8,128)(2,1)} %copy.104, f32[16,2048]{0,1:T(8,128)S(1)} %copy-done.25, f32[16,2048]{0,1:T(8,128)S(1)} %copy-done.15), kind=kOutput, calls=%fused_computation.103 | convolution fusion | flops 205520896 | bytes 3407872 | tf_op jit(solution)/shard_map/nqc,bqc->bnc/dot_general | solution.py:94
  887.9 5.1 copy.109
  895.1 18.6 %fusion.83 = f32[2048,8,64]{2,1,0:T(8,128)} fusion(bf16[8,64,2048]{1,0,2:T(8,128)(2,1)} %copy.104, bf16[64,64,2048]{1,0,2:T(8,128)(2,1)} %copy.84), kind=kOutput, calls=%fused_computation.150 | convolution fusion | flops 134217728 | bytes 23068672 | tf_op jit(solution)/shard_map/tsc,btc->bsc/dot_general | solution.py:105
  913.7 28.9 %collective-permute-done.6 = bf16[512,2048]{1,0:T(8,128)(2,1)} collective-permute-done((bf16[512,2048]{1,0:T(8,128)(2,1)}, bf16[512,2048]{1,0:T(8,128)(2,1)}, u32[]{:S(2)}, u32[]{:S(2)}) %collective-permute-start.6) | collective-permute-done | bytes 2097184 | tf_op jit(solution)/shard_map/ppermute | solution.py:21
  947.4 18.6 %fusion.84 = f32[2048,8,64]{2,1,0:T(8,128)} fusion(bf16[8,64,2048]{1,0,2:T(8,128)(2,1)} %copy.104, bf16[64,64,2048]{1,0,2:T(8,128)(2,1)} %copy.86), kind=kOutput, calls=%fused_computation.151 | convolution fusion | flops 134217728 | bytes 23068672 | tf_op jit(solution)/shard_map/tsc,btc->bsc/dot_general | solution.py:106
  972.5 25.4 %add_bitcast_fusion = f32[8,64,2048]{1,0,2:T(8,128)} fusion(f32[2048,8,64]{2,1,0:T(8,128)} %fusion.83, f32[2048,8,64]{2,1,0:T(8,128)} %fusion.84, f32[8,16,2048]{1,0,2:T(8,128)} %copy.110, f32[16,64,2048]{1,0,2:T(8,128)} %rev.4, f32[16,2048]{0,1:T(8,128)S(1)} %copy-done.13, f32[16,2048]{0,1:T(8,128)S(1)} %copy-done.8), kind=kOutput, calls=%fused_computation.72 | convolution fusion | flops 207618048 | bytes 22282240 | tf_op jit(solution)/shard_map/nqc,bnc->bqc/dot_general | solution.py:117
  997.8 7.0 copy.111
  1004.9 6.1 fusion.60
  (458 shorter events, 399.9 us)
Async XLA Ops:
  7.2 250.3 %all-gather.5.cloned.1.call-start = ((), (), s32[]{:S(2)}) async-start(), calls=%async_computation | async-start | bytes 1179648 | tf_op jit(solution)/shard_map/all_gather | solution.py:30
  7.2 406.7 %collective-permute-start = (bf16[512,2048]{1,0:T(8,128)(2,1)}, bf16[512,2048]{1,0:T(8,128)(2,1)}, u32[]{:S(2)}, u32[]{:S(2)}) collective-permute-start(bf16[512,2048]{1,0:T(8,128)(2,1)} %param.22), channel_id=1, source_target_pairs={{0,4},{4,8},{8,12},{12,16},{16,20},{20,24},{24,28},{1,5},{5,9},{9,... | collective-permute-start | bytes 6291464 | tf_op jit(solution)/shard_map/ppermute | solution.py:21
  10.6 406.5 %collective-permute-start.1 = (bf16[512,2048]{1,0:T(8,128)(2,1)}, bf16[512,2048]{1,0:T(8,128)(2,1)}, u32[]{:S(2)}, u32[]{:S(2)}) collective-permute-start(bf16[512,2048]{1,0:T(8,128)(2,1)} %param.22), channel_id=1, source_target_pairs={{0,8},{4,12},{8,16},{12,20},{16,24},{20,28},{1,9},{5,13},{9,17},{1... | collective-permute-start | bytes 6291464 | tf_op jit(solution)/shard_map/ppermute | solution.py:21
  22.3 236.7 %copy-start.21 = (f32[16,2048]{1,0:T(8,128)}, f32[16,2048]{1,0:T(8,128)S(1)}, u32[]{:S(2)}) copy-start(f32[16,2048]{1,0:T(8,128)S(1)} %get-tuple-element.550) | copy-start | bytes 393220
  22.6 242.5 %copy-start.14 = (f32[16,2048]{0,1:T(8,128)}, f32[16,2048]{0,1:T(8,128)S(1)}, u32[]{:S(2)}) copy-start(f32[16,2048]{0,1:T(8,128)S(1)} %copy.81) | copy-start | bytes 393220
  61.9 19.5 %copy-start.7 = (f32[16,2048]{0,1:T(8,128)}, f32[16,2048]{0,1:T(8,128)S(1)}, u32[]{:S(2)}) copy-start(f32[16,2048]{0,1:T(8,128)S(1)} %copy.87) | copy-start | bytes 393220
  95.8 21.3 %copy-start.5 = (f32[16,2048]{1,0:T(8,128)}, f32[16,2048]{1,0:T(8,128)S(1)}, u32[]{:S(2)}) copy-start(f32[16,2048]{1,0:T(8,128)S(1)} %get-tuple-element.956) | copy-start | bytes 393220
  95.8 21.3 %copy-start.18 = (f32[8,16,2048]{2,1,0:T(8,128)}, f32[8,16,2048]{2,1,0:T(8,128)S(1)}, u32[]{:S(2)}) copy-start(f32[8,16,2048]{2,1,0:T(8,128)S(1)} %get-tuple-element.267) | copy-start | bytes 3145732
  96.4 869.6 %all-gather.7.cloned.1.call-start = ((), (), s32[]{:S(2)}) async-start(), calls=%async_computation.1 | async-start | bytes 1179648 | tf_op jit(solution)/shard_map/all_gather | solution.py:30
  186.9 46.0 %copy-start.27 = (f32[16,2048]{1,0:T(8,128)S(1)}, f32[16,2048]{1,0:T(8,128)}, u32[]{:S(2)}) copy-start(f32[16,2048]{1,0:T(8,128)} %get-tuple-element.545) | copy-start | bytes 393220
  233.2 31.9 %copy-start.12 = (f32[16,2048]{0,1:T(8,128)}, f32[16,2048]{0,1:T(8,128)S(1)}, u32[]{:S(2)}) copy-start(f32[16,2048]{0,1:T(8,128)S(1)} %copy.91) | copy-start | bytes 393220
  233.2 24.3 %copy-start.23 = (f32[16,2048]{1,0:T(8,128)S(1)}, f32[16,2048]{1,0:T(8,128)}, u32[]{:S(2)}) copy-start(f32[16,2048]{1,0:T(8,128)} %get-tuple-element.549) | copy-start | bytes 393220
  294.8 7.2 copy-start.1
  302.0 8.8 copy-start.29
  310.9 10.0 copy-start.30
  310.9 11.9 %copy-start.19 = (bf16[512,2048]{1,0:T(8,128)(2,1)S(1)}, bf16[512,2048]{1,0:T(8,128)(2,1)}, u32[]{:S(2)}) copy-start(bf16[512,2048]{1,0:T(8,128)(2,1)} %param.22) | copy-start | bytes 6291460
  315.2 105.2 %collective-permute-start.5 = (bf16[512,2048]{1,0:T(8,128)(2,1)}, bf16[512,2048]{1,0:T(8,128)(2,1)}, u32[]{:S(2)}, u32[]{:S(2)}) collective-permute-start(bf16[512,2048]{1,0:T(8,128)(2,1)} %multiply_convert_fusion), channel_id=1, source_target_pairs={{0,8},{4,12},{8,16},{12,20},{16,24},{20,28},{1,9},{5,13},{9,17},{1... | collective-permute-start | bytes 6291464 | tf_op jit(solution)/shard_map/ppermute | solution.py:21
  318.6 101.7 %collective-permute-start.4 = (bf16[512,2048]{1,0:T(8,128)(2,1)}, bf16[512,2048]{1,0:T(8,128)(2,1)}, u32[]{:S(2)}, u32[]{:S(2)}) collective-permute-start(bf16[512,2048]{1,0:T(8,128)(2,1)} %multiply_convert_fusion), channel_id=1, source_target_pairs={{0,4},{4,8},{8,12},{12,16},{16,20},{20,24},{24,28},{1,5},{5,9},{9,... | collective-permute-start | bytes 6291464 | tf_op jit(solution)/shard_map/ppermute | solution.py:21
  320.8 43.6 %collective-permute-start.3 = (bf16[512]{0:T(512)(128)(2,1)S(1)}, bf16[512]{0:T(512)(128)(2,1)S(1)}, u32[]{:S(2)}, u32[]{:S(2)}) collective-permute-start(bf16[512]{0:T(512)(128)(2,1)S(1)} %add_convert_fusion.1), channel_id=1, source_target_pairs={{0,8},{4,12},{8,16},{12,20},{16,24},{20,28},{1,9},{5,13},{9,17},{1... | collective-permute-start | bytes 3080 | tf_op jit(solution)/shard_map/ppermute | solution.py:21
  364.4 49.5 %collective-permute-start.2 = (bf16[512]{0:T(512)(128)(2,1)S(1)}, bf16[512]{0:T(512)(128)(2,1)S(1)}, u32[]{:S(2)}, u32[]{:S(2)}) collective-permute-start(bf16[512]{0:T(512)(128)(2,1)S(1)} %add_convert_fusion.1), channel_id=1, source_target_pairs={{0,4},{4,8},{8,12},{12,16},{16,20},{20,24},{24,28},{1,5},{5,9},{9,... | collective-permute-start | bytes 3080 | tf_op jit(solution)/shard_map/ppermute | solution.py:21
  750.2 50.8 %collective-permute-start.9 = (bf16[512,2048]{1,0:T(8,128)(2,1)}, bf16[512,2048]{1,0:T(8,128)(2,1)}, u32[]{:S(2)}, u32[]{:S(2)}) collective-permute-start(bf16[512,2048]{1,0:T(8,128)(2,1)} %bitcast.122), channel_id=1, source_target_pairs={{8,0},{12,4},{16,8},{20,12},{24,16},{28,20},{9,1},{13,5},{17,9},{2... | collective-permute-start | bytes 6291464 | tf_op jit(solution)/shard_map/ppermute | solution.py:21
  754.0 89.4 %collective-permute-start.8 = (bf16[512,2048]{1,0:T(8,128)(2,1)}, bf16[512,2048]{1,0:T(8,128)(2,1)}, u32[]{:S(2)}, u32[]{:S(2)}) collective-permute-start(bf16[512,2048]{1,0:T(8,128)(2,1)} %bitcast.123), channel_id=1, source_target_pairs={{4,0},{8,4},{12,8},{16,12},{20,16},{24,20},{28,24},{5,1},{9,5},{13... | collective-permute-start | bytes 6291464 | tf_op jit(solution)/shard_map/ppermute | solution.py:21
  766.0 147.6 %collective-permute-start.7 = (bf16[512,2048]{1,0:T(8,128)(2,1)}, bf16[512,2048]{1,0:T(8,128)(2,1)}, u32[]{:S(2)}, u32[]{:S(2)}) collective-permute-start(bf16[512,2048]{1,0:T(8,128)(2,1)} %bitcast.125), channel_id=1, source_target_pairs={{8,0},{12,4},{16,8},{20,12},{24,16},{28,20},{9,1},{13,5},{17,9},{2... | collective-permute-start | bytes 6291464 | tf_op jit(solution)/shard_map/ppermute | solution.py:21
  769.9 172.7 %collective-permute-start.6 = (bf16[512,2048]{1,0:T(8,128)(2,1)}, bf16[512,2048]{1,0:T(8,128)(2,1)}, u32[]{:S(2)}, u32[]{:S(2)}) collective-permute-start(bf16[512,2048]{1,0:T(8,128)(2,1)} %bitcast.126), channel_id=1, source_target_pairs={{4,0},{8,4},{12,8},{16,12},{20,16},{24,20},{28,24},{5,1},{9,5},{13... | collective-permute-start | bytes 6291464 | tf_op jit(solution)/shard_map/ppermute | solution.py:21
  773.7 69.7 %copy-start = (f32[8,64,2048]{2,1,0:T(8,128)S(1)}, f32[8,64,2048]{2,1,0:T(8,128)}, u32[]{:S(2)}) copy-start(f32[8,64,2048]{2,1,0:T(8,128)} %copy.93) | copy-start | bytes 12582916
  774.3 69.1 %copy-start.2 = (bf16[16,64,8,128]{3,2,0,1:T(8,128)(2,1)}, bf16[16,64,8,128]{3,2,0,1:T(8,128)(2,1)S(1)}, u32[]{:S(2)}) copy-start(bf16[16,64,8,128]{3,2,0,1:T(8,128)(2,1)S(1)} %copy.132) | copy-start | bytes 6291460
  860.2 5.8 copy-start.25
  895.1 47.5 %copy-start.10 = (bf16[16,64,8,128]{3,2,0,1:T(8,128)(2,1)S(1)}, bf16[16,64,8,128]{3,2,0,1:T(8,128)(2,1)}, u32[]{:S(2)}) copy-start(bf16[16,64,8,128]{3,2,0,1:T(8,128)(2,1)} %copy.135) | copy-start | bytes 6291460
  947.4 18.6 %copy-start.24 = (f32[16,2048]{1,0:T(8,128)S(1)}, f32[16,2048]{1,0:T(8,128)}, u32[]{:S(2)}) copy-start(f32[16,2048]{1,0:T(8,128)} %get-tuple-element.549) | copy-start | bytes 393220
  947.4 20.1 %copy-start.17 = (f32[8,16,2048]{2,1,0:T(8,128)S(1)}, f32[8,16,2048]{2,1,0:T(8,128)}, u32[]{:S(2)}) copy-start(f32[8,16,2048]{2,1,0:T(8,128)} %copy-done.16) | copy-start | bytes 3145732
  947.4 20.1 %copy-start.22 = (f32[16,2048]{1,0:T(8,128)S(1)}, f32[16,2048]{1,0:T(8,128)}, u32[]{:S(2)}) copy-start(f32[16,2048]{1,0:T(8,128)} %copy-done.21) | copy-start | bytes 393220
  997.8 7.1 copy-start.9
  (11 other events, 39.6 us)
Sparse Core Ops, SparseCore 0:
  96.5 38.7 all-gather.4
  895.2 47.7 all-gather.6
where the time goes:
time: 1030 us; the launch traced here: 1020 us
  matrix products  446 us (43%)
  local copies, waits for them, and re-layouts  238 us (23%)
  waiting for transfers between devices  138 us (13%)
  other arithmetic  74.8 us (7%)
  starting transfers between devices  71.4 us (7%)
  loops' own time  22.6 us (2%)
  between operations  15.1 us (1%)
  blocking collectives  12.3 us (1%)
    ppermute x10, waiting for transfers between devices, shifted(): lax.ppermute(value, axis, [(source, source + steps) for source in range(i...  138 us
    dot_general x48, matrix products, pair_products(): lax.dot_general(left_rows, right_rows, (((1,), (1,)), ((), ())), preferre...  96.5 us
    dot_general x32, matrix products, column_products(): lax.dot_general(left_rows, right_rows, (((0,), (0,)), ((), ())), preferre...  73.4 us
    ppermute x10, starting transfers between devices, shifted(): lax.ppermute(value, axis, [(source, source + steps) for source in range(i...  71.1 us
    convert_element_type x1, local copies, waits for them, and re-layouts, filter_pieces(): (toeplitz - toeplitz_high.astype(jnp.float32)).astype(jnp.bfloat16)  46 us
    convert_element_type x1, local copies, waits for them, and re-layouts, filter_pieces(): toeplitz_high = toeplitz.astype(jnp.bfloat16)  46 us
    dot_general x16, matrix products, forward_head(): jnp.dot(weights_low, head_columns(values_all, head_index), preferred_elem...  40.9 us
    dot_general x16, matrix products, backward_head(): jnp.dot(dscore, key_rows, preferred_element_type=jnp.float32) * score_scale  35.7 us
  transfers between devices with their start and end apart: 12, of which 5 were waited for; matrix products, arithmetic and copies ran while one was open for 40% of the time, Pallas kernels for 0%

commit v1 on v0

v1 whole, which is shorter than its diff:
```python
import functools
import math

import jax
import jax.numpy as jnp
from jax import lax
from jax.experimental import pallas as pl
from jax.experimental.pallas import tpu as pltpu
from jax.sharding import PartitionSpec as P

D = 8192
HEAD_DIM = 128
SPAN = 2
EPS = 1e-06
NEG = -1e30
LANES = 128
SUB = 8
QUERY_BLOCK = 256
MOST = 1024
GROUPS = 4
VMEM = 56 * 1024 * 1024

F32 = jnp.float32
BF16 = jnp.bfloat16


def shifted(value, axis, steps):
    count = lax.axis_size(axis)
    initial, last = (max(0, -steps), min(count, count - steps))
    return lax.ppermute(value, axis, [(source, source + steps) for source in range(initial, last)])


def params():
    return pltpu.CompilerParams(vmem_limit_bytes=VMEM)


def spread(store, tokens, column):
    for j in range(SUB):
        store[pl.ds(j, tokens, SUB), :] = column(slice(j * LANES, (j + 1) * LANES))


def end_scan(signal, decay_ref, end_ref, tokens, backward):
    modes = decay_ref.shape[1]
    decays = [decay_ref[0, n] for n in range(modes)]

    def step(s, states):
        t = tokens - 1 - s if backward else s
        x = signal[pl.ds(pl.multiple_of(t * SUB, SUB), SUB), :]
        return tuple(decays[n] * states[n] + x for n in range(modes))

    zero = jnp.zeros((SUB, LANES), F32)
    states = lax.fori_loop(0, tokens, step, (zero,) * modes, unroll=8)
    for n in range(modes):
        end_ref[0, n] = states[n]


def full_scan(signal, decay_ref, weight_ref, state_ref, tokens, backward):
    modes = decay_ref.shape[1]
    decays = [decay_ref[0, n] for n in range(modes)]
    weights = [weight_ref[0, n] for n in range(modes)]

    def step(s, states):
        t = tokens - 1 - s if backward else s
        rows = pl.ds(pl.multiple_of(t * SUB, SUB), SUB)
        x = signal[rows, :]
        states = tuple(decays[n] * states[n] + x for n in range(modes))
        terms = [weights[n] * states[n] for n in range(modes)]
        while len(terms) > 1:
            terms = [terms[i] + terms[i + 1] for i in range(0, len(terms), 2)]
        signal[rows, :] = terms[0]
        return states

    lax.fori_loop(0, tokens, step, tuple(state_ref[0, n] for n in range(modes)), unroll=4)


def forward_ends(k_ref, v_ref, decay_ref, end_ref, signal):
    tokens = k_ref.shape[0]
    spread(signal, tokens, lambda c: (k_ref[:, c].astype(F32) * v_ref[:, c].astype(F32)).astype(BF16).astype(F32))
    end_scan(signal, decay_ref, end_ref, tokens, False)


def forward_mix(k_ref, v_ref, q_ref, decay_ref, weight_ref, state_ref, mixed_ref, power_ref, signal):
    tokens = k_ref.shape[0]
    spread(signal, tokens, lambda c: (k_ref[:, c].astype(F32) * v_ref[:, c].astype(F32)).astype(BF16).astype(F32))
    full_scan(signal, decay_ref, weight_ref, state_ref, tokens, False)
    power = jnp.zeros((tokens, LANES), F32)
    for j in range(SUB):
        c = slice(j * LANES, (j + 1) * LANES)
        mixed = signal[pl.ds(j, tokens, SUB), :]
        mixed_ref[:, c] = mixed
        lifted = q_ref[:, c].astype(F32) * mixed
        power = power + lifted * lifted

    @pl.when(pl.program_id(0) == 0)
    def _():
        power_ref[...] = power

    @pl.when(pl.program_id(0) > 0)
    def _():
        power_ref[...] += power


def backward_ends(g_ref, decay_ref, end_ref, signal):
    tokens = g_ref.shape[0]
    spread(signal, tokens, lambda c: g_ref[:, c].astype(F32))
    end_scan(signal, decay_ref, end_ref, tokens, True)


def backward_mix(g_ref, k_ref, v_ref, decay_ref, weight_ref, state_ref, dk_ref, dv_ref, signal):
    tokens = k_ref.shape[0]
    spread(signal, tokens, lambda c: g_ref[:, c].astype(F32))
    full_scan(signal, decay_ref, weight_ref, state_ref, tokens, True)
    for j in range(SUB):
        c = slice(j * LANES, (j + 1) * LANES)
        grad = signal[pl.ds(j, tokens, SUB), :]
        dk_ref[:, c] = (grad * v_ref[:, c].astype(F32)).astype(BF16)
        dv_ref[:, c] = (grad * k_ref[:, c].astype(F32)).astype(BF16)


def conv_call(body, name, tokens, channels, modes, in_kinds, out_kinds, flops, arrays):
    width = SUB * LANES
    specs = {
        "wide": pl.BlockSpec((tokens, width), lambda i: (0, i)),
        "mode": pl.BlockSpec((1, modes, SUB, LANES), lambda i: (i, 0, 0, 0)),
        "row": pl.BlockSpec((tokens, LANES), lambda i: (0, 0)),
    }
    shapes = {
        "wide": (tokens, channels),
        "mode": (channels // width, modes, SUB, LANES),
        "row": (tokens, LANES),
    }
    return pl.pallas_call(
        body,
        grid=(channels // width,),
        in_specs=[specs[kind] for kind in in_kinds],
        out_specs=[specs[kind] for kind, _ in out_kinds],
        out_shape=[jax.ShapeDtypeStruct(shapes[kind], dtype) for kind, dtype in out_kinds],
        scratch_shapes=[pltpu.VMEM((tokens * SUB, LANES), F32)],
        compiler_params=params(),
        cost_estimate=pl.CostEstimate(
            flops=flops * tokens * channels * modes, bytes_accessed=12 * tokens * channels, transcendentals=0
        ),
        name=name,
    )(*arrays)


def carried_state(slab_rate, local_state, backward):
    slab_count = lax.axis_size("ctx")
    collected = lax.all_gather(local_state[None], "ctx", axis=0, tiled=True)
    position = lax.axis_index("ctx")
    others = jnp.arange(slab_count, dtype=jnp.int32)
    spacing = others - position - 1 if backward else position - 1 - others
    spacing = spacing.reshape((slab_count,) + (1,) * local_state.ndim)
    distances = jnp.maximum(spacing, 0).astype(F32)
    weights = jnp.where(spacing >= 0, jnp.exp(-slab_rate[None] * distances), 0.0)
    return jnp.sum(weights * collected, axis=0)


def dots(left, right, a, b):
    return lax.dot_general(left, right, (((a,), (b,)), ((), ())), preferred_element_type=F32)


def attention(count, tokens, span, chained, first_ref, start_ref, *refs):
    ins, refs = refs[: 4 + 2 * span], refs[4 + 2 * span :]
    if chained:
        refs = refs[2:]
    q_ref, g_ref = ins[:2]
    key_refs, value_refs = ins[2 : 3 + span], ins[3 + span :]
    out_ref, dq_ref = refs[:2]
    dk_refs, dv_refs = refs[2 : 3 + span], refs[3 + span : 4 + 2 * span]
    bias, keys, values, dkeys, dvalues = refs[4 + 2 * span :]
    total = (span + 1) * tokens
    base = span * tokens
    scale = HEAD_DIM ** (-0.5)
    rate = scale * math.log2(math.e)

    @pl.when(pl.program_id(0) == 0)
    def _():
        for low in range(0, total, tokens):
            place = low + lax.broadcasted_iota(jnp.int32, (tokens, tokens), 0)
            row = base + lax.broadcasted_iota(jnp.int32, (tokens, tokens), 1)
            allowed = (place >= start_ref[...]) & (place <= row)
            bias[low : low + tokens, :] = jnp.where(allowed, 0.0, NEG)

    for j in range(span + 1):
        keys[j * tokens : (j + 1) * tokens, :] = key_refs[j][...]
        values[j * tokens : (j + 1) * tokens, :] = value_refs[j][...]
    dkeys[...] = jnp.zeros_like(dkeys)
    dvalues[...] = jnp.zeros_like(dvalues)

    size = QUERY_BLOCK
    for block in range(tokens // size):
        rows = slice(block * size, (block + 1) * size)
        stop = base + (block + 1) * size
        most = min((MOST + size) // size, stop // size)

        def variant(pieces, rows=rows, stop=stop):
            span_keys = slice(stop - pieces * size, stop)
            q = q_ref[rows, :]
            g = g_ref[rows, :]
            k = keys[span_keys, :]
            v = values[span_keys, :]
            scores = dots(k, q, 1, 1) + bias[span_keys, rows]
            top = jnp.max(scores, axis=0, keepdims=True)
            exponent = jnp.exp2((scores - top) * rate)
            probs = exponent * (1.0 / jnp.sum(exponent, axis=0, keepdims=True))
            low = probs.astype(BF16)
            output = dots(v, low, 0, 0)
            delta = jnp.sum(g.astype(F32).T * output, axis=0, keepdims=True)
            dscore = (probs * (dots(v, g, 1, 1) - delta)).astype(BF16)
            out_ref[rows, :] = output.T.astype(BF16)
            dq_ref[rows, :] = (dots(k, dscore, 0, 0) * scale).T.astype(BF16)
            dkeys[span_keys, :] += dots(dscore, q, 1, 0)
            dvalues[span_keys, :] += dots(low, g, 1, 0)

        needed = stop // size - first_ref[block]
        for pieces in range(1, most + 1):
            hit = needed == pieces if pieces < most else needed >= pieces
            pl.when(hit)(functools.partial(variant, pieces))

    for j in range(span + 1):
        part = slice(j * tokens, (j + 1) * tokens)
        dk_refs[j][...] = (dkeys[part, :] * scale).astype(BF16)
        dv_refs[j][...] = dvalues[part, :].astype(BF16)


def attend(group, count, first, start, q_att, cotangent, key_list, value_list, previous):
    tokens, channels = q_att.shape
    span = len(key_list) - 1
    heads = count // HEAD_DIM
    offset = group * heads
    whole = pl.BlockSpec((tokens, HEAD_DIM), lambda h, f: (0, offset + h))
    piece = pl.BlockSpec((tokens, HEAD_DIM), lambda h, f: (0, h))
    ins = [pl.BlockSpec((1, tokens), lambda h, f: (0, 0)), whole, whole]
    for entry in key_list + value_list:
        ins.append(whole if entry.shape[1] == channels else piece)
    aliases = {}
    operands = [first, start, q_att, cotangent, *key_list, *value_list]
    if previous is not None:
        ins += [pl.BlockSpec(memory_space=pl.ANY)] * 2
        aliases = {len(operands): 0, len(operands) + 1: 1}
        operands += list(previous)
    wide = jax.ShapeDtypeStruct((tokens, channels), BF16)
    small = jax.ShapeDtypeStruct((tokens, count), BF16)
    total = (span + 1) * tokens
    results = pl.pallas_call(
        functools.partial(attention, count, tokens, span, previous is not None),
        grid_spec=pltpu.PrefetchScalarGridSpec(
            num_scalar_prefetch=1,
            grid=(heads,),
            in_specs=ins,
            out_specs=[whole, whole] + [piece] * (2 * span + 2),
            scratch_shapes=[
                pltpu.VMEM((total, tokens), F32),
                pltpu.VMEM((total, HEAD_DIM), BF16),
                pltpu.VMEM((total, HEAD_DIM), BF16),
                pltpu.VMEM((total, HEAD_DIM), F32),
                pltpu.VMEM((total, HEAD_DIM), F32),
            ],
        ),
        out_shape=[wide, wide] + [small] * (2 * span + 2),
        input_output_aliases=aliases,
        compiler_params=params(),
        cost_estimate=pl.CostEstimate(
            flops=12 * heads * tokens * total * HEAD_DIM,
            bytes_accessed=32 * tokens * count,
            transcendentals=heads * tokens * total,
        ),
        name=f"attention_{group}",
    )(*operands)
    return results[:2], results[2 : 3 + span], results[3 + span :]


def local(q_li, k_li, v_li, q_att, k_att, cotangent, record_ids, decay_rate, residue, norm_gain):
    tokens, channels = q_li.shape
    modes = decay_rate.shape[0]
    width = SUB * LANES
    groups = math.gcd(GROUPS, channels // HEAD_DIM)
    count = channels // groups

    def by_group(array):
        return jnp.transpose(array.reshape(modes, channels // width, SUB, LANES), (1, 0, 2, 3))

    rate = by_group(decay_rate)
    decay = jnp.exp(-rate)
    weight = by_group(residue) * jnp.sqrt(-jnp.expm1(-2.0 * rate))
    slab_rate = rate * tokens
    call = functools.partial(conv_call, tokens=tokens, channels=channels, modes=modes)

    marks = record_ids + 1
    all_marks = [shifted(marks, "ctx", d) for d in range(SPAN, 0, -1)] + [marks]
    all_marks = jnp.concatenate(all_marks)
    start = jnp.sum((all_marks[:, None] < marks[None, :]).astype(jnp.int32), axis=0)
    first = start[::QUERY_BLOCK] // QUERY_BLOCK
    start = start[None, :]

    cols = [slice(g * count, (g + 1) * count) for g in range(groups)]
    far_keys = [[shifted(k_att[:, c], "ctx", d) for d in range(SPAN, 0, -1)] for c in cols]

    (ends,) = call(
        forward_ends, "forward_ends", in_kinds=("wide", "wide", "mode"), out_kinds=(("mode", F32),),
        flops=2, arrays=(k_li, v_li, decay),
    )
    incoming = carried_state(slab_rate, ends, False)
    mixed, power = call(
        forward_mix, "forward_mix", in_kinds=("wide",) * 3 + ("mode",) * 3,
        out_kinds=(("wide", F32), ("row", F32)), flops=4,
        arrays=(k_li, v_li, q_li, decay, weight, incoming),
    )
    inv_rms = lax.rsqrt(lax.psum(jnp.sum(power, axis=1), "ch") / D + EPS)[:, None]
    gain = norm_gain[None, :]

    previous = None
    key_totals, value_totals = [], []
    for g, c in enumerate(cols):
        values = (q_li[:, c].astype(F32) * mixed[:, c] * inv_rms * gain[:, c]).astype(BF16)
        far_values = [shifted(values, "ctx", d) for d in range(SPAN, 0, -1)]
        previous, dks, dvs = attend(
            g, count, first, start, q_att, cotangent, far_keys[g] + [k_att], far_values + [values], previous
        )
        key_total = dks[SPAN].astype(F32)
        value_total = dvs[SPAN].astype(F32)
        for d in range(1, SPAN + 1):
            key_total = key_total + shifted(dks[SPAN - d], "ctx", -d).astype(F32)
            value_total = value_total + shifted(dvs[SPAN - d], "ctx", -d).astype(F32)
        key_totals.append(key_total.astype(BF16))
        value_totals.append(value_total)
    attended, d_q_att = previous
    d_k_att = jnp.concatenate(key_totals, axis=1)
    inner = jnp.zeros((tokens,), F32)
    for c, value_total in zip(cols, value_totals):
        lifted = q_li[:, c].astype(F32) * mixed[:, c]
        inner = inner + jnp.sum(lifted * value_total * gain[:, c], axis=1)
    inner = lax.psum(inner, "ch")[:, None]
    weighted = jnp.concatenate(value_totals, axis=1) * gain
    query = q_li.astype(F32)
    lifted_grad = inv_rms * weighted - query * mixed * (inv_rms**3) * inner / D
    d_q_li = (lifted_grad * mixed).astype(BF16)
    mixed_grad = (lifted_grad * query).astype(BF16)
    (starts,) = call(
        backward_ends, "backward_ends", in_kinds=("wide", "mode"), out_kinds=(("mode", F32),),
        flops=2, arrays=(mixed_grad, decay),
    )
    arriving = carried_state(slab_rate, starts, True)
    d_k_li, d_v_li = call(
        backward_mix, "backward_mix", in_kinds=("wide",) * 3 + ("mode",) * 3,
        out_kinds=(("wide", BF16), ("wide", BF16)), flops=4,
        arrays=(mixed_grad, k_li, v_li, decay, weight, arriving),
    )
    return (attended, d_q_att, d_k_att, d_q_li, d_k_li, d_v_li)


def solution(mesh):
    wide = P("ctx", "ch")
    return jax.shard_map(
        local,
        mesh=mesh,
        in_specs=(wide,) * 6 + (P("ctx"), P(None, "ch"), P(None, "ch"), P("ch")),
        out_specs=(wide,) * 6,
        check_vma=False,
    )
```

time: 1030 us -> 501 us (0.49)
  matrix products: 446 us -> 0 us
  local copies, waits for them, and re-layouts: 238 us -> 3.56 us
  Pallas kernels: 0 us -> 108 us
  waiting for transfers between devices: 138 us -> 228 us
  other arithmetic: 74.8 us -> 26 us
  starting transfers between devices: 71.4 us -> 103 us
  loops' own time: 22.6 us -> 0 us
    dot_general x121 -> x0, matrix products: 446 us -> none  [the longest x48 96.5 us: pair_products(): lax.dot_general(left_rows, right_rows, (((1,), (1,)), ((), ())), preferre...]
    pallas_call x0 -> x8, Pallas kernels: none -> 108 us  [the longest x4 58.8 us: attend(): pl.pallas_call(functools.partial(attention, count, tokens, span, previous...]
    convert_element_type x8 -> x0, local copies, waits for them, and re-layouts: 102 us -> none  [the longest x1 46 us: filter_pieces(): (toeplitz - toeplitz_high.astype(jnp.float32)).astype(jnp.bfloat16)]
    ppermute x10 -> x34, waiting for transfers between devices: 138 us -> 198 us  [shifted(): lax.ppermute(value, axis, [(source, source + steps) for source in range(i...]
    dynamic_slice x96 -> x0, local copies, waits for them, and re-layouts: 35.6 us -> none  [the longest x32 18.8 us: local(): lax.map(forward_head, head_numbers)]
    ppermute x10 -> x34, starting transfers between devices: 71.1 us -> 103 us  [shifted(): lax.ppermute(value, axis, [(source, source + steps) for source in range(i...]
    all_gather x2, waiting for transfers between devices: 0.01 us -> 29.1 us  [carried_state(): collected = lax.all_gather(local_state[None], 'ctx', axis=0, tiled=True)]
    unnamed x69 -> x45, local copies, waits for them, and re-layouts: 28.3 us -> 0.96 us
  transfers between devices with their start and end apart: 12 -> 36, of which waited for: 5 -> 21; matrix products, arithmetic and copies ran while one was open for 40% -> 5% of each run, Pallas kernels for 0% -> 14%
where the time goes in v1:
time: 501 us; the launch traced here: 497 us
  waiting for transfers between devices  228 us (46%)
  Pallas kernels  108 us (22%)
  starting transfers between devices  103 us (21%)
  other arithmetic  26 us (5%)
  between operations  15.1 us (3%)
  blocking collectives  12.8 us (3%)
    ppermute x34, waiting for transfers between devices, shifted(): lax.ppermute(value, axis, [(source, source + steps) for source in range(i...  198 us
    ppermute x34, starting transfers between devices, shifted(): lax.ppermute(value, axis, [(source, source + steps) for source in range(i...  103 us
    pallas_call x4, Pallas kernels, attend(): pl.pallas_call(functools.partial(attention, count, tokens, span, previous...  58.8 us
    pallas_call x4, Pallas kernels, conv_call(): pl.pallas_call(body, grid=(channels // width,), in_specs=[specs[kind] for...  49.4 us
    all_gather x2, waiting for transfers between devices, carried_state(): collected = lax.all_gather(local_state[None], 'ctx', axis=0, tiled=True)  29.1 us
  transfers between devices with their start and end apart: 36, of which 21 were waited for; matrix products, arithmetic and copies ran while one was open for 5% of the time, Pallas kernels for 14%

profile of v1, /device:TPU:8, one launch (start us, length us, event | category | flops | bytes accessed | tf_op | source)
XLA Modules:
  0.0 496.6 jit_solution(8239670346616630639)
XLA Ops:
  9.1 8.3 %forward_ends.1 = f32[2,16,8,128]{3,2,1,0:T(8,128)} custom-call(bf16[512,2048]{1,0:T(8,128)(2,1)} %k_ref.5, bf16[512,2048]{1,0:T(8,128)(2,1)} %v_ref.5, f32[2,16,8,128]{3,2,1,0:T(8,128)} %bitcast.28), custom_call_target="tpu_custom_call" | custom-call | flops 33554432 | bytes 12582912 | tf_op jit(solution)/shard_map/forward_ends/pallas_call | solution.py:132
  33.7 29.1 %all-gather.5.cloned.1.call-done = f32[16,16,8,128]{3,2,1,0:T(8,128)} async-done(((f32[2,16,8,128]{3,2,1,0:T(8,128)}), f32[16,16,8,128]{3,2,1,0:T(8,128)}) %all-gather.5.cloned.1.call-update) | async-done | bytes 1048592 | tf_op jit(solution)/shard_map/all_gather | solution.py:149
  65.1 16.0 %forward_mix.1 = (f32[512,2048]{1,0:T(8,128)}, f32[512,128]{1,0:T(8,128)}) custom-call(bf16[512,2048]{1,0:T(8,128)(2,1)} %k_ref.5, bf16[512,2048]{1,0:T(8,128)(2,1)} %v_ref.5, bf16[512,2048]{1,0:T(8,128)(2,1)} %q_ref.1, f32[2,16,8,128]{3,2,1,0:T(8,128)} %bitcast.29, f32[2,16,8,128]{3,2,1,0:T(8,128)} %bitcast.34, ...), custom_call_target="tpu_custom_call" | custom-call | flops 67108864 | bytes 12582912 | tf_op jit(solution)/shard_map/forward_mix/pallas_call | solution.py:132
  82.1 7.1 %psum.14 = f32[512]{0:T(512)S(1)} all-reduce(f32[512]{0:T(512)S(1)} %reduce_sum.74), channel_id=1, replica_groups=mesh['ctx'=8,'ch'=4] {'ch'}, use_global_device_ids=true, to_apply=%region_3.4 | all-reduce | flops 512 | bytes 4096 | tf_op jit(solution)/shard_map/psum | solution.py:310
  114.3 10.8 %collective-permute-start.13 = (bf16[512,512]{1,0:T(8,128)(2,1)}, bf16[512,512]{1,0:T(8,128)(2,1)S(1)}, u32[]{:S(2)}, u32[]{:S(2)}) collective-permute-start(bf16[512,512]{1,0:T(8,128)(2,1)} %get-tuple-element.89.refs_7_), channel_id=1, source_target_pairs={{0,4},{4,8},{8,12},{12,16},{16,20},{20,24},{24,28},{1,5},{5,9},{9,... | collective-permute-start | bytes 1572872 | tf_op jit(solution)/shard_map/ppermute | solution.py:30
  128.7 16.5 %collective-permute-done.17.refs_6_ = bf16[512,512]{1,0:T(8,128)(2,1)} collective-permute-done((bf16[512,512]{1,0:T(8,128)(2,1)}, bf16[512,512]{1,0:T(8,128)(2,1)}, u32[]{:S(2)}, u32[]{:S(2)}) %collective-permute-start.17) | collective-permute-done | bytes 524320 | tf_op jit(solution)/shard_map/ppermute | solution.py:30
  147.1 14.5 %attention_0.1 = (bf16[512,2048]{1,0:T(8,128)(2,1)}, bf16[512,2048]{1,0:T(8,128)(2,1)}, bf16[512,512]{1,0:T(8,128)(2,1)}, bf16[512,512]{1,0:T(8,128)(2,1)}, bf16...) custom-call(s32[2]{0:T(128)} %and_select_fusion.first_ref, ...), custom_call_target="tpu_custom_call" | custom-call | flops 4831838208 | bytes 8388608 | tf_op jit(solution)/shard_map/attention_0/pallas_call | solution.py:246
  165.0 5.3 %collective-permute-start.3 = (bf16[512,512]{1,0:T(8,128)(2,1)S(1)}, bf16[512,512]{1,0:T(8,128)(2,1)S(1)}, u32[]{:S(2)}, u32[]{:S(2)}) collective-permute-start(bf16[512,512]{1,0:T(8,128)(2,1)S(1)} %get-tuple-element.95), channel_id=1, source_target_pairs={{0,4},{4,8},{8,12},{12,16},{16,20},{20,24},{24,28},{1,5},{5,9},{9,... | collective-permute-start | bytes 1572872 | tf_op jit(solution)/shard_map/ppermute | solution.py:30
  170.3 8.5 %collective-permute-done.13.refs_6_ = bf16[512,512]{1,0:T(8,128)(2,1)S(1)} collective-permute-done((bf16[512,512]{1,0:T(8,128)(2,1)}, bf16[512,512]{1,0:T(8,128)(2,1)S(1)}, u32[]{:S(2)}, u32[]{:S(2)}) %collective-permute-start.13) | collective-permute-done | bytes 524320 | tf_op jit(solution)/shard_map/ppermute | solution.py:30
  181.6 10.8 %collective-permute-start.5 = (bf16[512,512]{1,0:T(8,128)(2,1)S(1)}, bf16[512,512]{1,0:T(8,128)(2,1)}, u32[]{:S(2)}, u32[]{:S(2)}) collective-permute-start(bf16[512,512]{1,0:T(8,128)(2,1)S(1)} %copy-done.7), channel_id=1, source_target_pairs={{0,4},{4,8},{8,12},{12,16},{16,20},{20,24},{24,28},{1,5},{5,9},{9,... | collective-permute-start | bytes 1572872 | tf_op jit(solution)/shard_map/ppermute | solution.py:30
  192.5 14.7 %attention_1.1 = (bf16[512,2048]{1,0:T(8,128)(2,1)}, bf16[512,2048]{1,0:T(8,128)(2,1)}, bf16[512,512]{1,0:T(8,128)(2,1)}, bf16[512,512]{1,0:T(8,128)(2,1)}, bf16...) custom-call(s32[2]{0:T(128)} %and_select_fusion.first_ref, ...), custom_call_target="tpu_custom_call", output_to_operand_aliasing={{0}: (10, {}), {1}: (11, {})} | custom-call | flops 4831838208 | bytes 8388608 | tf_op jit(solution)/shard_map/attention_1/pallas_call | solution.py:246
  208.0 14.3 %attention_2.1 = (bf16[512,2048]{1,0:T(8,128)(2,1)}, bf16[512,2048]{1,0:T(8,128)(2,1)}, bf16[512,512]{1,0:T(8,128)(2,1)}, bf16[512,512]{1,0:T(8,128)(2,1)}, bf16...) custom-call(s32[2]{0:T(128)} %and_select_fusion.first_ref, ...), custom_call_target="tpu_custom_call", output_to_operand_aliasing={{0}: (10, {}), {1}: (11, {})} | custom-call | flops 4831838208 | bytes 8388608 | tf_op jit(solution)/shard_map/attention_2/pallas_call | solution.py:246
  223.7 20.1 %collective-permute-done.5.refs_6_ = bf16[512,512]{1,0:T(8,128)(2,1)} collective-permute-done((bf16[512,512]{1,0:T(8,128)(2,1)S(1)}, bf16[512,512]{1,0:T(8,128)(2,1)}, u32[]{:S(2)}, u32[]{:S(2)}) %collective-permute-start.5) | collective-permute-done | bytes 524320 | tf_op jit(solution)/shard_map/ppermute | solution.py:30
  243.8 15.3 %attention_3.1 = (bf16[512,2048]{1,0:T(8,128)(2,1)}, bf16[512,2048]{1,0:T(8,128)(2,1)}, bf16[512,512]{1,0:T(8,128)(2,1)}, bf16[512,512]{1,0:T(8,128)(2,1)}, bf16...) custom-call(s32[2]{0:T(128)} %and_select_fusion.first_ref, ...), custom_call_target="tpu_custom_call", output_to_operand_aliasing={{0}: (10, {}), {1}: (11, {})} | custom-call | flops 4831838208 | bytes 8388608 | tf_op jit(solution)/shard_map/attention_3/pallas_call | solution.py:246
  268.7 7.3 %collective-permute-done.32 = bf16[512,512]{1,0:T(8,128)(2,1)S(1)} collective-permute-done((bf16[512,512]{1,0:T(8,128)(2,1)}, bf16[512,512]{1,0:T(8,128)(2,1)S(1)}, u32[]{:S(2)}, u32[]{:S(2)}) %collective-permute-start.32) | collective-permute-done | bytes 524320 | tf_op jit(solution)/shard_map/ppermute | solution.py:30
  278.0 8.3 %collective-permute-done.33 = bf16[512,512]{1,0:T(8,128)(2,1)S(1)} collective-permute-done((bf16[512,512]{1,0:T(8,128)(2,1)}, bf16[512,512]{1,0:T(8,128)(2,1)S(1)}, u32[]{:S(2)}, u32[]{:S(2)}) %collective-permute-start.33) | collective-permute-done | bytes 524320 | tf_op jit(solution)/shard_map/ppermute | solution.py:30
  288.2 8.0 %collective-permute-done.30 = bf16[512,512]{1,0:T(8,128)(2,1)S(1)} collective-permute-done((bf16[512,512]{1,0:T(8,128)(2,1)}, bf16[512,512]{1,0:T(8,128)(2,1)S(1)}, u32[]{:S(2)}, u32[]{:S(2)}) %collective-permute-start.30) | collective-permute-done | bytes 524320 | tf_op jit(solution)/shard_map/ppermute | solution.py:30
  298.1 10.6 %collective-permute-done.31 = bf16[512,512]{1,0:T(8,128)(2,1)S(1)} collective-permute-done((bf16[512,512]{1,0:T(8,128)(2,1)}, bf16[512,512]{1,0:T(8,128)(2,1)S(1)}, u32[]{:S(2)}, u32[]{:S(2)}) %collective-permute-start.31) | collective-permute-done | bytes 524320 | tf_op jit(solution)/shard_map/ppermute | solution.py:30
  310.6 8.0 %collective-permute-done.28 = bf16[512,512]{1,0:T(8,128)(2,1)S(1)} collective-permute-done((bf16[512,512]{1,0:T(8,128)(2,1)}, bf16[512,512]{1,0:T(8,128)(2,1)S(1)}, u32[]{:S(2)}, u32[]{:S(2)}) %collective-permute-start.28) | collective-permute-done | bytes 524320 | tf_op jit(solution)/shard_map/ppermute | solution.py:30
  320.6 10.6 %collective-permute-done.29 = bf16[512,512]{1,0:T(8,128)(2,1)S(1)} collective-permute-done((bf16[512,512]{1,0:T(8,128)(2,1)}, bf16[512,512]{1,0:T(8,128)(2,1)S(1)}, u32[]{:S(2)}, u32[]{:S(2)}) %collective-permute-start.29) | collective-permute-done | bytes 524320 | tf_op jit(solution)/shard_map/ppermute | solution.py:30
  331.2 9.8 %collective-permute-done.26 = bf16[512,512]{1,0:T(8,128)(2,1)S(1)} collective-permute-done((bf16[512,512]{1,0:T(8,128)(2,1)S(1)}, bf16[512,512]{1,0:T(8,128)(2,1)S(1)}, u32[]{:S(2)}, u32[]{:S(2)}) %collective-permute-start.26) | collective-permute-done | bytes 524320 | tf_op jit(solution)/shard_map/ppermute | solution.py:30
  341.0 12.6 %collective-permute-done.27 = bf16[512,512]{1,0:T(8,128)(2,1)S(1)} collective-permute-done((bf16[512,512]{1,0:T(8,128)(2,1)S(1)}, bf16[512,512]{1,0:T(8,128)(2,1)S(1)}, u32[]{:S(2)}, u32[]{:S(2)}) %collective-permute-start.27) | collective-permute-done | bytes 524320 | tf_op jit(solution)/shard_map/ppermute | solution.py:30
  353.7 4.4 multiply_reduce_fusion.3
  358.1 5.7 %psum.15 = f32[512]{0:T(512)S(1)} all-reduce(f32[512]{0:T(512)S(1)} %add_add_fusion), channel_id=1, replica_groups=mesh['ctx'=8,'ch'=4] {'ch'}, use_global_device_ids=true, to_apply=%region_8.9 | all-reduce | flops 512 | bytes 4096 | tf_op jit(solution)/shard_map/psum | solution.py:334
  363.8 6.0 %fusion.4 = (bf16[512,2048]{1,0:T(8,128)(2,1)}, bf16[512,2048]{1,0:T(8,128)(2,1)}) fusion(bf16[512,2048]{1,0:T(8,128)(2,1)S(1)} %copy-done.1, f32[512]{0:T(512)S(1)} %psum.15, f32[512]{0:T(512)S(1)} %get-tuple-element.103, f32[512,2048]{1,0:T(8,128)} %get-tuple-element.42, f32[2048]{0:T(1024)S(1)} %copy-done.8, f32[512,512]{1,0:T(8,128)S(1)} %get-tuple-element.82, ...), kind=kLoop, calls=%fused_computation.6 | loop fusion | flops 15728640 | bytes 14694400 | tf_op jit(solution)/shard_map/convert_element_type | solution.py:339
  369.8 7.9 %backward_ends.1 = f32[2,16,8,128]{3,2,1,0:T(8,128)} custom-call(bf16[512,2048]{1,0:T(8,128)(2,1)} %get-tuple-element.86.g_ref, f32[2,16,8,128]{3,2,1,0:T(8,128)} %bitcast.30), custom_call_target="tpu_custom_call" | custom-call | flops 33554432 | bytes 12582912 | tf_op jit(solution)/shard_map/backward_ends/pallas_call | solution.py:132
  390.9 4.5 collective-permute-done.20
  398.9 20.5 %collective-permute-done.21 = bf16[512,512]{1,0:T(8,128)(2,1)S(1)} collective-permute-done((bf16[512,512]{1,0:T(8,128)(2,1)}, bf16[512,512]{1,0:T(8,128)(2,1)S(1)}, u32[]{:S(2)}, u32[]{:S(2)}) %collective-permute-start.21) | collective-permute-done | bytes 524320 | tf_op jit(solution)/shard_map/ppermute | solution.py:30
  419.6 5.8 %collective-permute-done.22 = bf16[512,512]{1,0:T(8,128)(2,1)S(1)} collective-permute-done((bf16[512,512]{1,0:T(8,128)(2,1)}, bf16[512,512]{1,0:T(8,128)(2,1)S(1)}, u32[]{:S(2)}, u32[]{:S(2)}) %collective-permute-start.22) | collective-permute-done | bytes 524320 | tf_op jit(solution)/shard_map/ppermute | solution.py:30
  425.4 21.0 %collective-permute-done.23 = bf16[512,512]{1,0:T(8,128)(2,1)S(1)} collective-permute-done((bf16[512,512]{1,0:T(8,128)(2,1)}, bf16[512,512]{1,0:T(8,128)(2,1)S(1)}, u32[]{:S(2)}, u32[]{:S(2)}) %collective-permute-start.23) | collective-permute-done | bytes 524320 | tf_op jit(solution)/shard_map/ppermute | solution.py:30
  449.8 18.3 %collective-permute-done.25 = bf16[512,512]{1,0:T(8,128)(2,1)S(1)} collective-permute-done((bf16[512,512]{1,0:T(8,128)(2,1)}, bf16[512,512]{1,0:T(8,128)(2,1)S(1)}, u32[]{:S(2)}, u32[]{:S(2)}) %collective-permute-start.25) | collective-permute-done | bytes 524320 | tf_op jit(solution)/shard_map/ppermute | solution.py:30
  472.1 17.2 %backward_mix.1 = (bf16[512,2048]{1,0:T(8,128)(2,1)}, bf16[512,2048]{1,0:T(8,128)(2,1)}) custom-call(bf16[512,2048]{1,0:T(8,128)(2,1)} %get-tuple-element.86.g_ref, bf16[512,2048]{1,0:T(8,128)(2,1)} %k_ref.5, bf16[512,2048]{1,0:T(8,128)(2,1)} %v_ref.5, f32[2,16,8,128]{3,2,1,0:T(8,128)} %bitcast.31, f32[2,16,8,128]{3,2,1,0:T(8,128)} %bitcast.35, ...), custom_call_target="tpu_custom_call" | custom-call | flops 67108864 | bytes 12582912 | tf_op jit(solution)/shard_map/backward_mix/pallas_call | solution.py:132
  (124 shorter events, 103.6 us)
Async XLA Ops:
  7.2 55.7 %all-gather.5.cloned.1.call-start = ((), (), s32[]{:S(2)}) async-start(), calls=%async_computation | async-start | bytes 1179648 | tf_op jit(solution)/shard_map/all_gather | solution.py:149
  17.4 452.5 %all-gather.7.cloned.1.call-start = ((), (), s32[]{:S(2)}) async-start(), calls=%async_computation.1 | async-start | bytes 1179648 | tf_op jit(solution)/shard_map/all_gather | solution.py:149
  17.5 76.0 %collective-permute-start = (s32[512]{0:T(512)S(1)}, s32[512]{0:T(512)S(1)}, u32[]{:S(2)}, u32[]{:S(2)}) collective-permute-start(s32[512]{0:T(512)S(1)} %broadcast_add_fusion), channel_id=1, source_target_pairs={{0,8},{4,12},{8,16},{12,20},{16,24},{20,28},{1,9},{5,13},{9,17},{1... | collective-permute-start | bytes 6152 | tf_op jit(solution)/shard_map/ppermute | solution.py:30
  21.0 76.2 %collective-permute-start.1 = (s32[512]{0:T(512)S(1)}, s32[512]{0:T(512)S(1)}, u32[]{:S(2)}, u32[]{:S(2)}) collective-permute-start(s32[512]{0:T(512)S(1)} %broadcast_add_fusion), channel_id=1, source_target_pairs={{0,4},{4,8},{8,12},{12,16},{16,20},{20,24},{24,28},{1,5},{5,9},{9,... | collective-permute-start | bytes 6152 | tf_op jit(solution)/shard_map/ppermute | solution.py:30
  25.6 74.3 %collective-permute-start.14 = (bf16[512,512]{1,0:T(8,128)(2,1)}, bf16[512,512]{1,0:T(8,128)(2,1)}, u32[]{:S(2)}, u32[]{:S(2)}) collective-permute-start(bf16[512,512]{1,0:T(8,128)(2,1)} %get-tuple-element.92), channel_id=1, source_target_pairs={{0,8},{4,12},{8,16},{12,20},{16,24},{20,28},{1,9},{5,13},{9,17},{1... | collective-permute-start | bytes 1572872 | tf_op jit(solution)/shard_map/ppermute | solution.py:30
  29.1 73.5 %collective-permute-start.15 = (bf16[512,512]{1,0:T(8,128)(2,1)}, bf16[512,512]{1,0:T(8,128)(2,1)}, u32[]{:S(2)}, u32[]{:S(2)}) collective-permute-start(bf16[512,512]{1,0:T(8,128)(2,1)} %get-tuple-element.92), channel_id=1, source_target_pairs={{0,4},{4,8},{8,12},{12,16},{16,20},{20,24},{24,28},{1,5},{5,9},{9,... | collective-permute-start | bytes 1572872 | tf_op jit(solution)/shard_map/ppermute | solution.py:30
  31.0 75.5 %collective-permute-start.10 = (bf16[512,512]{1,0:T(8,128)(2,1)}, bf16[512,512]{1,0:T(8,128)(2,1)}, u32[]{:S(2)}, u32[]{:S(2)}) collective-permute-start(bf16[512,512]{1,0:T(8,128)(2,1)} %get-tuple-element.93), channel_id=1, source_target_pairs={{0,8},{4,12},{8,16},{12,20},{16,24},{20,28},{1,9},{5,13},{9,17},{1... | collective-permute-start | bytes 1572872 | tf_op jit(solution)/shard_map/ppermute | solution.py:30
  99.9 25.6 %collective-permute-start.16 = (bf16[512,512]{1,0:T(8,128)(2,1)}, bf16[512,512]{1,0:T(8,128)(2,1)}, u32[]{:S(2)}, u32[]{:S(2)}) collective-permute-start(bf16[512,512]{1,0:T(8,128)(2,1)} %get-tuple-element.88.refs_7_), channel_id=1, source_target_pairs={{0,8},{4,12},{8,16},{12,20},{16,24},{20,28},{1,9},{5,13},{9,17},{1... | collective-permute-start | bytes 1572872 | tf_op jit(solution)/shard_map/ppermute | solution.py:30
  102.6 42.5 %collective-permute-start.17 = (bf16[512,512]{1,0:T(8,128)(2,1)}, bf16[512,512]{1,0:T(8,128)(2,1)}, u32[]{:S(2)}, u32[]{:S(2)}) collective-permute-start(bf16[512,512]{1,0:T(8,128)(2,1)} %get-tuple-element.88.refs_7_), channel_id=1, source_target_pairs={{0,4},{4,8},{8,12},{12,16},{16,20},{20,24},{24,28},{1,5},{5,9},{9,... | collective-permute-start | bytes 1572872 | tf_op jit(solution)/shard_map/ppermute | solution.py:30
  106.5 55.0 %collective-permute-start.7 = (bf16[512,512]{1,0:T(8,128)(2,1)}, bf16[512,512]{1,0:T(8,128)(2,1)S(1)}, u32[]{:S(2)}, u32[]{:S(2)}) collective-permute-start(bf16[512,512]{1,0:T(8,128)(2,1)} %get-tuple-element.94), channel_id=1, source_target_pairs={{0,4},{4,8},{8,12},{12,16},{16,20},{20,24},{24,28},{1,5},{5,9},{9,... | collective-permute-start | bytes 1572872 | tf_op jit(solution)/shard_map/ppermute | solution.py:30
  111.4 53.5 %collective-permute-start.12 = (bf16[512,512]{1,0:T(8,128)(2,1)}, bf16[512,512]{1,0:T(8,128)(2,1)S(1)}, u32[]{:S(2)}, u32[]{:S(2)}) collective-permute-start(bf16[512,512]{1,0:T(8,128)(2,1)} %get-tuple-element.89.refs_7_), channel_id=1, source_target_pairs={{0,8},{4,12},{8,16},{12,20},{16,24},{20,28},{1,9},{5,13},{9,17},{1... | collective-permute-start | bytes 1572872 | tf_op jit(solution)/shard_map/ppermute | solution.py:30
  114.3 64.4 %collective-permute-start.13 = (bf16[512,512]{1,0:T(8,128)(2,1)}, bf16[512,512]{1,0:T(8,128)(2,1)S(1)}, u32[]{:S(2)}, u32[]{:S(2)}) collective-permute-start(bf16[512,512]{1,0:T(8,128)(2,1)} %get-tuple-element.89.refs_7_), channel_id=1, source_target_pairs={{0,4},{4,8},{8,12},{12,16},{16,20},{20,24},{24,28},{1,5},{5,9},{9,... | collective-permute-start | bytes 1572872 | tf_op jit(solution)/shard_map/ppermute | solution.py:30
  125.5 56.1 %collective-permute-start.8 = (bf16[512,512]{1,0:T(8,128)(2,1)}, bf16[512,512]{1,0:T(8,128)(2,1)S(1)}, u32[]{:S(2)}, u32[]{:S(2)}) collective-permute-start(bf16[512,512]{1,0:T(8,128)(2,1)} %get-tuple-element.90.refs_7_), channel_id=1, source_target_pairs={{0,8},{4,12},{8,16},{12,20},{16,24},{20,28},{1,9},{5,13},{9,17},{1... | collective-permute-start | bytes 1572872 | tf_op jit(solution)/shard_map/ppermute | solution.py:30
  145.1 62.0 %collective-permute-start.9 = (bf16[512,512]{1,0:T(8,128)(2,1)}, bf16[512,512]{1,0:T(8,128)(2,1)S(1)}, u32[]{:S(2)}, u32[]{:S(2)}) collective-permute-start(bf16[512,512]{1,0:T(8,128)(2,1)} %get-tuple-element.90.refs_7_), channel_id=1, source_target_pairs={{0,4},{4,8},{8,12},{12,16},{16,20},{20,24},{24,28},{1,5},{5,9},{9,... | collective-permute-start | bytes 1572872 | tf_op jit(solution)/shard_map/ppermute | solution.py:30
  161.6 60.7 %collective-permute-start.2 = (bf16[512,512]{1,0:T(8,128)(2,1)S(1)}, bf16[512,512]{1,0:T(8,128)(2,1)S(1)}, u32[]{:S(2)}, u32[]{:S(2)}) collective-permute-start(bf16[512,512]{1,0:T(8,128)(2,1)S(1)} %get-tuple-element.95), channel_id=1, source_target_pairs={{0,8},{4,12},{8,16},{12,20},{16,24},{20,28},{1,9},{5,13},{9,17},{1... | collective-permute-start | bytes 1572872 | tf_op jit(solution)/shard_map/ppermute | solution.py:30
  165.0 58.7 %collective-permute-start.3 = (bf16[512,512]{1,0:T(8,128)(2,1)S(1)}, bf16[512,512]{1,0:T(8,128)(2,1)S(1)}, u32[]{:S(2)}, u32[]{:S(2)}) collective-permute-start(bf16[512,512]{1,0:T(8,128)(2,1)S(1)} %get-tuple-element.95), channel_id=1, source_target_pairs={{0,4},{4,8},{8,12},{12,16},{16,20},{20,24},{24,28},{1,5},{5,9},{9,... | collective-permute-start | bytes 1572872 | tf_op jit(solution)/shard_map/ppermute | solution.py:30
  178.8 44.9 %collective-permute-start.4 = (bf16[512,512]{1,0:T(8,128)(2,1)S(1)}, bf16[512,512]{1,0:T(8,128)(2,1)S(1)}, u32[]{:S(2)}, u32[]{:S(2)}) collective-permute-start(bf16[512,512]{1,0:T(8,128)(2,1)S(1)} %copy-done.7), channel_id=1, source_target_pairs={{0,8},{4,12},{8,16},{12,20},{16,24},{20,28},{1,9},{5,13},{9,17},{1... | collective-permute-start | bytes 1572872 | tf_op jit(solution)/shard_map/ppermute | solution.py:30
  181.6 62.1 %collective-permute-start.5 = (bf16[512,512]{1,0:T(8,128)(2,1)S(1)}, bf16[512,512]{1,0:T(8,128)(2,1)}, u32[]{:S(2)}, u32[]{:S(2)}) collective-permute-start(bf16[512,512]{1,0:T(8,128)(2,1)S(1)} %copy-done.7), channel_id=1, source_target_pairs={{0,4},{4,8},{8,12},{12,16},{16,20},{20,24},{24,28},{1,5},{5,9},{9,... | collective-permute-start | bytes 1572872 | tf_op jit(solution)/shard_map/ppermute | solution.py:30
  261.0 25.2 %collective-permute-start.33 = (bf16[512,512]{1,0:T(8,128)(2,1)}, bf16[512,512]{1,0:T(8,128)(2,1)S(1)}, u32[]{:S(2)}, u32[]{:S(2)}) collective-permute-start(bf16[512,512]{1,0:T(8,128)(2,1)} %get-tuple-element.75), channel_id=1, source_target_pairs={{8,0},{12,4},{16,8},{20,12},{24,16},{28,20},{9,1},{13,5},{17,9},{2... | collective-permute-start | bytes 1572872 | tf_op jit(solution)/shard_map/ppermute | solution.py:30
  262.9 33.2 %collective-permute-start.30 = (bf16[512,512]{1,0:T(8,128)(2,1)}, bf16[512,512]{1,0:T(8,128)(2,1)S(1)}, u32[]{:S(2)}, u32[]{:S(2)}) collective-permute-start(bf16[512,512]{1,0:T(8,128)(2,1)} %get-tuple-element.71), channel_id=1, source_target_pairs={{4,0},{8,4},{12,8},{16,12},{20,16},{24,20},{28,24},{5,1},{9,5},{13... | collective-permute-start | bytes 1572872 | tf_op jit(solution)/shard_map/ppermute | solution.py:30
  264.9 43.8 %collective-permute-start.31 = (bf16[512,512]{1,0:T(8,128)(2,1)}, bf16[512,512]{1,0:T(8,128)(2,1)S(1)}, u32[]{:S(2)}, u32[]{:S(2)}) collective-permute-start(bf16[512,512]{1,0:T(8,128)(2,1)} %get-tuple-element.72), channel_id=1, source_target_pairs={{8,0},{12,4},{16,8},{20,12},{24,16},{28,20},{9,1},{13,5},{17,9},{2... | collective-permute-start | bytes 1572872 | tf_op jit(solution)/shard_map/ppermute | solution.py:30
  266.8 51.8 %collective-permute-start.28 = (bf16[512,512]{1,0:T(8,128)(2,1)}, bf16[512,512]{1,0:T(8,128)(2,1)S(1)}, u32[]{:S(2)}, u32[]{:S(2)}) collective-permute-start(bf16[512,512]{1,0:T(8,128)(2,1)} %get-tuple-element.68), channel_id=1, source_target_pairs={{4,0},{8,4},{12,8},{16,12},{20,16},{24,20},{28,24},{5,1},{9,5},{13... | collective-permute-start | bytes 1572872 | tf_op jit(solution)/shard_map/ppermute | solution.py:30
  276.1 55.1 %collective-permute-start.29 = (bf16[512,512]{1,0:T(8,128)(2,1)}, bf16[512,512]{1,0:T(8,128)(2,1)S(1)}, u32[]{:S(2)}, u32[]{:S(2)}) collective-permute-start(bf16[512,512]{1,0:T(8,128)(2,1)} %get-tuple-element.69), channel_id=1, source_target_pairs={{8,0},{12,4},{16,8},{20,12},{24,16},{28,20},{9,1},{13,5},{17,9},{2... | collective-permute-start | bytes 1572872 | tf_op jit(solution)/shard_map/ppermute | solution.py:30
  286.2 54.8 %collective-permute-start.26 = (bf16[512,512]{1,0:T(8,128)(2,1)S(1)}, bf16[512,512]{1,0:T(8,128)(2,1)S(1)}, u32[]{:S(2)}, u32[]{:S(2)}) collective-permute-start(bf16[512,512]{1,0:T(8,128)(2,1)S(1)} %copy-done.12), channel_id=1, source_target_pairs={{4,0},{8,4},{12,8},{16,12},{20,16},{24,20},{28,24},{5,1},{9,5},{13... | collective-permute-start | bytes 1572872 | tf_op jit(solution)/shard_map/ppermute | solution.py:30
  296.2 57.5 %collective-permute-start.27 = (bf16[512,512]{1,0:T(8,128)(2,1)S(1)}, bf16[512,512]{1,0:T(8,128)(2,1)S(1)}, u32[]{:S(2)}, u32[]{:S(2)}) collective-permute-start(bf16[512,512]{1,0:T(8,128)(2,1)S(1)} %copy-done.11), channel_id=1, source_target_pairs={{8,0},{12,4},{16,8},{20,12},{24,16},{28,20},{9,1},{13,5},{17,9},{2... | collective-permute-start | bytes 1572872 | tf_op jit(solution)/shard_map/ppermute | solution.py:30
  308.7 76.7 %collective-permute-start.18 = (bf16[512,512]{1,0:T(8,128)(2,1)}, bf16[512,512]{1,0:T(8,128)(2,1)}, u32[]{:S(2)}, u32[]{:S(2)}) collective-permute-start(bf16[512,512]{1,0:T(8,128)(2,1)} %get-tuple-element.53), channel_id=1, source_target_pairs={{4,0},{8,4},{12,8},{16,12},{20,16},{24,20},{28,24},{5,1},{9,5},{13... | collective-permute-start | bytes 1572872 | tf_op jit(solution)/shard_map/ppermute | solution.py:30
  318.6 68.8 %collective-permute-start.19 = (bf16[512,512]{1,0:T(8,128)(2,1)}, bf16[512,512]{1,0:T(8,128)(2,1)}, u32[]{:S(2)}, u32[]{:S(2)}) collective-permute-start(bf16[512,512]{1,0:T(8,128)(2,1)} %get-tuple-element.54), channel_id=1, source_target_pairs={{8,0},{12,4},{16,8},{20,12},{24,16},{28,20},{9,1},{13,5},{17,9},{2... | collective-permute-start | bytes 1572872 | tf_op jit(solution)/shard_map/ppermute | solution.py:30
  379.7 39.7 %collective-permute-start.21 = (bf16[512,512]{1,0:T(8,128)(2,1)}, bf16[512,512]{1,0:T(8,128)(2,1)S(1)}, u32[]{:S(2)}, u32[]{:S(2)}) collective-permute-start(bf16[512,512]{1,0:T(8,128)(2,1)} %get-tuple-element.57), channel_id=1, source_target_pairs={{8,0},{12,4},{16,8},{20,12},{24,16},{28,20},{9,1},{13,5},{17,9},{2... | collective-permute-start | bytes 1572872 | tf_op jit(solution)/shard_map/ppermute | solution.py:30
  382.1 43.3 %collective-permute-start.22 = (bf16[512,512]{1,0:T(8,128)(2,1)}, bf16[512,512]{1,0:T(8,128)(2,1)S(1)}, u32[]{:S(2)}, u32[]{:S(2)}) collective-permute-start(bf16[512,512]{1,0:T(8,128)(2,1)} %get-tuple-element.59), channel_id=1, source_target_pairs={{4,0},{8,4},{12,8},{16,12},{20,16},{24,20},{28,24},{5,1},{9,5},{13... | collective-permute-start | bytes 1572872 | tf_op jit(solution)/shard_map/ppermute | solution.py:30
  385.5 61.0 %collective-permute-start.23 = (bf16[512,512]{1,0:T(8,128)(2,1)}, bf16[512,512]{1,0:T(8,128)(2,1)S(1)}, u32[]{:S(2)}, u32[]{:S(2)}) collective-permute-start(bf16[512,512]{1,0:T(8,128)(2,1)} %get-tuple-element.60), channel_id=1, source_target_pairs={{8,0},{12,4},{16,8},{20,12},{24,16},{28,20},{9,1},{13,5},{17,9},{2... | collective-permute-start | bytes 1572872 | tf_op jit(solution)/shard_map/ppermute | solution.py:30
  387.4 62.5 %collective-permute-start.24 = (bf16[512,512]{1,0:T(8,128)(2,1)}, bf16[512,512]{1,0:T(8,128)(2,1)S(1)}, u32[]{:S(2)}, u32[]{:S(2)}) collective-permute-start(bf16[512,512]{1,0:T(8,128)(2,1)} %get-tuple-element.62), channel_id=1, source_target_pairs={{4,0},{8,4},{12,8},{16,12},{20,16},{24,20},{28,24},{5,1},{9,5},{13... | collective-permute-start | bytes 1572872 | tf_op jit(solution)/shard_map/ppermute | solution.py:30
  395.4 72.7 %collective-permute-start.25 = (bf16[512,512]{1,0:T(8,128)(2,1)}, bf16[512,512]{1,0:T(8,128)(2,1)S(1)}, u32[]{:S(2)}, u32[]{:S(2)}) collective-permute-start(bf16[512,512]{1,0:T(8,128)(2,1)} %get-tuple-element.63), channel_id=1, source_target_pairs={{8,0},{12,4},{16,8},{20,12},{24,16},{28,20},{9,1},{13,5},{17,9},{2... | collective-permute-start | bytes 1572872 | tf_op jit(solution)/shard_map/ppermute | solution.py:30
  (25 other events, 963.5 us)
Sparse Core Ops, SparseCore 0:
  17.6 45.2 all-gather.4
  377.9 54.5 all-gather.6

commit v2 on v1

--- a/solution.py
+++ b/solution.py
@@ -17,7 +17,6 @@
 SUB = 8
 QUERY_BLOCK = 256
 MOST = 1024
-GROUPS = 4
 VMEM = 56 * 1024 * 1024
 
 F32 = jnp.float32
@@ -160,47 +159,105 @@
     return lax.dot_general(left, right, (((a,), (b,)), ((), ())), preferred_element_type=F32)
 
 
-def attention(count, tokens, span, chained, first_ref, start_ref, *refs):
-    ins, refs = refs[: 4 + 2 * span], refs[4 + 2 * span :]
-    if chained:
-        refs = refs[2:]
-    q_ref, g_ref = ins[:2]
-    key_refs, value_refs = ins[2 : 3 + span], ins[3 + span :]
-    out_ref, dq_ref = refs[:2]
-    dk_refs, dv_refs = refs[2 : 3 + span], refs[3 + span : 4 + 2 * span]
-    bias, keys, values, dkeys, dvalues = refs[4 + 2 * span :]
+def attention(tokens, heads, slabs, span, start_ref, q_ref, g_ref, *refs):
+    key_refs, refs = refs[: span + 1], refs[span + 1 :]
+    own_values, out_ref, dq_ref, dk_ref, dv_ref = refs[:5]
+    bias, keys, values, dkeys, dvalues, far_values, sent, landed, own = refs[5:14]
+    value_send, value_recv, grad_send, grad_recv = refs[14:]
     total = (span + 1) * tokens
     base = span * tokens
     scale = HEAD_DIM ** (-0.5)
     rate = scale * math.log2(math.e)
-
-    @pl.when(pl.program_id(0) == 0)
+    step = pl.program_id(0)
+    me = lax.axis_index("ctx")
+    distances = range(span, 0, -1)
+
+    def value_copy(d, h):
+        return pltpu.make_async_remote_copy(
+            src_ref=own_values.at[:, pl.ds(pl.multiple_of(h * HEAD_DIM, HEAD_DIM), HEAD_DIM)],
+            dst_ref=far_values.at[d - 1, h],
+            send_sem=value_send.at[d - 1, h],
+            recv_sem=value_recv.at[d - 1, h],
+            device_id={"ctx": lax.rem(me + d, slabs)},
+            device_id_type=pl.DeviceIdType.MESH,
+        )
+
+    def grad_copy(kind, d, h):
+        return pltpu.make_async_remote_copy(
+            src_ref=sent.at[kind, d - 1, h],
+            dst_ref=landed.at[kind, d - 1, h],
+            send_sem=grad_send.at[kind, d - 1, h],
+            recv_sem=grad_recv.at[kind, d - 1, h],
+            device_id={"ctx": lax.rem(me - d + slabs, slabs)},
+            device_id_type=pl.DeviceIdType.MESH,
+        )
+
+    @pl.when(step == 0)
     def _():
+        barrier = pltpu.get_barrier_semaphore()
+        partners = 0
+        for d in distances:
+            later, earlier = me + d < slabs, me >= d
+
+            @pl.when(later)
+            def _(d=d):
+                pl.semaphore_signal(
+                    barrier, inc=1, device_id={"ctx": lax.rem(me + d, slabs)}, device_id_type=pl.DeviceIdType.MESH
+                )
+
+            @pl.when(earlier)
+            def _(d=d):
+                pl.semaphore_signal(
+                    barrier,
+                    inc=1,
+                    device_id={"ctx": lax.rem(me - d + slabs, slabs)},
+                    device_id_type=pl.DeviceIdType.MESH,
+                )
+
+            partners = partners + later.astype(jnp.int32) + earlier.astype(jnp.int32)
+        pl.semaphore_wait(barrier, partners)
+
+        @pl.loop(0, heads)
+        def _(h):
+            for d in distances:
+                pl.when(me + d < slabs)(lambda d=d: value_copy(d, h).start())
+
         for low in range(0, total, tokens):
             place = low + lax.broadcasted_iota(jnp.int32, (tokens, tokens), 0)
             row = base + lax.broadcasted_iota(jnp.int32, (tokens, tokens), 1)
             allowed = (place >= start_ref[...]) & (place <= row)
             bias[low : low + tokens, :] = jnp.where(allowed, 0.0, NEG)
 
-    for j in range(span + 1):
-        keys[j * tokens : (j + 1) * tokens, :] = key_refs[j][...]
-        values[j * tokens : (j + 1) * tokens, :] = value_refs[j][...]
-    dkeys[...] = jnp.zeros_like(dkeys)
-    dvalues[...] = jnp.zeros_like(dvalues)
-
-    size = QUERY_BLOCK
-    for block in range(tokens // size):
-        rows = slice(block * size, (block + 1) * size)
-        stop = base + (block + 1) * size
-        most = min((MOST + size) // size, stop // size)
-
-        def variant(pieces, rows=rows, stop=stop):
-            span_keys = slice(stop - pieces * size, stop)
+    @pl.when(step < heads)
+    def _():
+        h = jnp.minimum(step, heads - 1)
+        for d in distances:
+            slab = slice((span - d) * tokens, (span - d + 1) * tokens)
+
+            @pl.when(me >= d)
+            def _(d=d, slab=slab):
+                value_copy(d, h).wait_recv()
+                values[slab, :] = far_values[d - 1, h]
+
+            @pl.when(me < d)
+            def _(d=d, slab=slab):
+                values[slab, :] = jnp.zeros((tokens, HEAD_DIM), BF16)
+
+        values[base:, :] = own_values[:, pl.ds(pl.multiple_of(h * HEAD_DIM, HEAD_DIM), HEAD_DIM)]
+        for j in range(span + 1):
+            keys[j * tokens : (j + 1) * tokens, :] = key_refs[j][...]
+        dkeys[...] = jnp.zeros_like(dkeys)
+        dvalues[...] = jnp.zeros_like(dvalues)
+        size = QUERY_BLOCK
+        for block in range(tokens // size):
+            rows = slice(block * size, (block + 1) * size)
+            stop = base + (block + 1) * size
+            near = slice(max(0, stop - MOST - size), stop)
             q = q_ref[rows, :]
             g = g_ref[rows, :]
-            k = keys[span_keys, :]
-            v = values[span_keys, :]
-            scores = dots(k, q, 1, 1) + bias[span_keys, rows]
+            k = keys[near, :]
+            v = values[near, :]
+            scores = dots(k, q, 1, 1) + bias[near, rows]
             top = jnp.max(scores, axis=0, keepdims=True)
             exponent = jnp.exp2((scores - top) * rate)
             probs = exponent * (1.0 / jnp.sum(exponent, axis=0, keepdims=True))
@@ -210,73 +267,98 @@
             dscore = (probs * (dots(v, g, 1, 1) - delta)).astype(BF16)
             out_ref[rows, :] = output.T.astype(BF16)
             dq_ref[rows, :] = (dots(k, dscore, 0, 0) * scale).T.astype(BF16)
-            dkeys[span_keys, :] += dots(dscore, q, 1, 0)
-            dvalues[span_keys, :] += dots(low, g, 1, 0)
-
-        needed = stop // size - first_ref[block]
-        for pieces in range(1, most + 1):
-            hit = needed == pieces if pieces < most else needed >= pieces
-            pl.when(hit)(functools.partial(variant, pieces))
-
-    for j in range(span + 1):
-        part = slice(j * tokens, (j + 1) * tokens)
-        dk_refs[j][...] = (dkeys[part, :] * scale).astype(BF16)
-        dv_refs[j][...] = dvalues[part, :].astype(BF16)
-
-
-def attend(group, count, first, start, q_att, cotangent, key_list, value_list, previous):
+            dkeys[near, :] += dots(dscore, q, 1, 0)
+            dvalues[near, :] += dots(low, g, 1, 0)
+
+        for d in range(span, -1, -1):
+            slab = slice((span - d) * tokens, (span - d + 1) * tokens)
+            key_part = (dkeys[slab, :] * scale).astype(BF16)
+            value_part = dvalues[slab, :].astype(BF16)
+            if d == 0:
+                own[0, h] = key_part
+                own[1, h] = value_part
+                continue
+
+            @pl.when(me >= d)
+            def _(d=d, key_part=key_part, value_part=value_part):
+                sent[0, d - 1, h] = key_part
+                sent[1, d - 1, h] = value_part
+                grad_copy(0, d, h).start()
+                grad_copy(1, d, h).start()
+
+    @pl.when(step >= heads)
+    def _():
+        h = jnp.maximum(step - heads, 0)
+        for d in distances:
+
+            @pl.when(me + d < slabs)
+            def _(d=d):
+                value_copy(d, h).wait_send()
+                grad_copy(0, d, h).wait_recv()
+                grad_copy(1, d, h).wait_recv()
+
+            @pl.when(me + d >= slabs)
+            def _(d=d):
+                for kind in range(2):
+                    landed[kind, d - 1, h] = jnp.zeros((tokens, HEAD_DIM), BF16)
+
+            @pl.when(me >= d)
+            def _(d=d):
+                grad_copy(0, d, h).wait_send()
+                grad_copy(1, d, h).wait_send()
+
+        sums = [own[kind, h].astype(F32) for kind in range(2)]
+        for d in range(1, span + 1):
+            sums = [sums[kind] + landed[kind, d - 1, h].astype(F32) for kind in range(2)]
+        dk_ref[...] = sums[0].astype(BF16)
+        dv_ref[...] = sums[1]
+
+
+def attend(start, q_att, cotangent, key_list, values, slabs):
     tokens, channels = q_att.shape
     span = len(key_list) - 1
-    heads = count // HEAD_DIM
-    offset = group * heads
-    whole = pl.BlockSpec((tokens, HEAD_DIM), lambda h, f: (0, offset + h))
-    piece = pl.BlockSpec((tokens, HEAD_DIM), lambda h, f: (0, h))
-    ins = [pl.BlockSpec((1, tokens), lambda h, f: (0, 0)), whole, whole]
-    for entry in key_list + value_list:
-        ins.append(whole if entry.shape[1] == channels else piece)
-    aliases = {}
-    operands = [first, start, q_att, cotangent, *key_list, *value_list]
-    if previous is not None:
-        ins += [pl.BlockSpec(memory_space=pl.ANY)] * 2
-        aliases = {len(operands): 0, len(operands) + 1: 1}
-        operands += list(previous)
-    wide = jax.ShapeDtypeStruct((tokens, channels), BF16)
-    small = jax.ShapeDtypeStruct((tokens, count), BF16)
+    heads = channels // HEAD_DIM
+    first = pl.BlockSpec((tokens, HEAD_DIM), lambda h: (0, jnp.minimum(h, heads - 1)))
+    second = pl.BlockSpec((tokens, HEAD_DIM), lambda h: (0, jnp.maximum(h - heads, 0)))
     total = (span + 1) * tokens
-    results = pl.pallas_call(
-        functools.partial(attention, count, tokens, span, previous is not None),
-        grid_spec=pltpu.PrefetchScalarGridSpec(
-            num_scalar_prefetch=1,
-            grid=(heads,),
-            in_specs=ins,
-            out_specs=[whole, whole] + [piece] * (2 * span + 2),
-            scratch_shapes=[
-                pltpu.VMEM((total, tokens), F32),
-                pltpu.VMEM((total, HEAD_DIM), BF16),
-                pltpu.VMEM((total, HEAD_DIM), BF16),
-                pltpu.VMEM((total, HEAD_DIM), F32),
-                pltpu.VMEM((total, HEAD_DIM), F32),
-            ],
-        ),
-        out_shape=[wide, wide] + [small] * (2 * span + 2),
-        input_output_aliases=aliases,
-        compiler_params=params(),
+    low = jax.ShapeDtypeStruct((tokens, channels), BF16)
+    return pl.pallas_call(
+        functools.partial(attention, tokens, heads, slabs, span),
+        grid=(2 * heads,),
+        in_specs=[pl.BlockSpec((1, tokens), lambda h: (0, 0))]
+        + [first] * (3 + span)
+        + [pl.BlockSpec(memory_space=pltpu.VMEM)],
+        out_specs=[first, first, second, second],
+        out_shape=[low, low, low, jax.ShapeDtypeStruct((tokens, channels), F32)],
+        scratch_shapes=[
+            pltpu.VMEM((total, tokens), F32),
+            pltpu.VMEM((total, HEAD_DIM), BF16),
+            pltpu.VMEM((total, HEAD_DIM), BF16),
+            pltpu.VMEM((total, HEAD_DIM), F32),
+            pltpu.VMEM((total, HEAD_DIM), F32),
+            pltpu.VMEM((span, heads, tokens, HEAD_DIM), BF16),
+            pltpu.VMEM((2, span, heads, tokens, HEAD_DIM), BF16),
+            pltpu.VMEM((2, span, heads, tokens, HEAD_DIM), BF16),
+            pltpu.VMEM((2, heads, tokens, HEAD_DIM), BF16),
+            pltpu.SemaphoreType.DMA((span, heads)),
+            pltpu.SemaphoreType.DMA((span, heads)),
+            pltpu.SemaphoreType.DMA((2, span, heads)),
+            pltpu.SemaphoreType.DMA((2, span, heads)),
+        ],
+        compiler_params=pltpu.CompilerParams(vmem_limit_bytes=VMEM, collective_id=0, has_side_effects=True),
         cost_estimate=pl.CostEstimate(
             flops=12 * heads * tokens * total * HEAD_DIM,
-            bytes_accessed=32 * tokens * count,
+            bytes_accessed=32 * tokens * channels,
             transcendentals=heads * tokens * total,
         ),
-        name=f"attention_{group}",
-    )(*operands)
-    return results[:2], results[2 : 3 + span], results[3 + span :]
+        name="attention",
+    )(start, q_att, cotangent, *key_list, values)
 
 
 def local(q_li, k_li, v_li, q_att, k_att, cotangent, record_ids, decay_rate, residue, norm_gain):
     tokens, channels = q_li.shape
     modes = decay_rate.shape[0]
     width = SUB * LANES
-    groups = math.gcd(GROUPS, channels // HEAD_DIM)
-    count = channels // groups
 
     def by_group(array):
         return jnp.transpose(array.reshape(modes, channels // width, SUB, LANES), (1, 0, 2, 3))
@@ -291,11 +373,8 @@
     all_marks = [shifted(marks, "ctx", d) for d in range(SPAN, 0, -1)] + [marks]
     all_marks = jnp.concatenate(all_marks)
     start = jnp.sum((all_marks[:, None] < marks[None, :]).astype(jnp.int32), axis=0)
-    first = start[::QUERY_BLOCK] // QUERY_BLOCK
     start = start[None, :]
-
-    cols = [slice(g * count, (g + 1) * count) for g in range(groups)]
-    far_keys = [[shifted(k_att[:, c], "ctx", d) for d in range(SPAN, 0, -1)] for c in cols]
+    key_list = [shifted(k_att, "ctx", d) for d in range(SPAN, 0, -1)] + [k_att]
 
     (ends,) = call(
         forward_ends, "forward_ends", in_kinds=("wide", "wide", "mode"), out_kinds=(("mode", F32),),
@@ -310,29 +389,12 @@
     inv_rms = lax.rsqrt(lax.psum(jnp.sum(power, axis=1), "ch") / D + EPS)[:, None]
     gain = norm_gain[None, :]
 
-    previous = None
-    key_totals, value_totals = [], []
-    for g, c in enumerate(cols):
-        values = (q_li[:, c].astype(F32) * mixed[:, c] * inv_rms * gain[:, c]).astype(BF16)
-        far_values = [shifted(values, "ctx", d) for d in range(SPAN, 0, -1)]
-        previous, dks, dvs = attend(
-            g, count, first, start, q_att, cotangent, far_keys[g] + [k_att], far_values + [values], previous
-        )
-        key_total = dks[SPAN].astype(F32)
-        value_total = dvs[SPAN].astype(F32)
-        for d in range(1, SPAN + 1):
-            key_total = key_total + shifted(dks[SPAN - d], "ctx", -d).astype(F32)
-            value_total = value_total + shifted(dvs[SPAN - d], "ctx", -d).astype(F32)
-        key_totals.append(key_total.astype(BF16))
-        value_totals.append(value_total)
-    attended, d_q_att = previous
-    d_k_att = jnp.concatenate(key_totals, axis=1)
-    inner = jnp.zeros((tokens,), F32)
-    for c, value_total in zip(cols, value_totals):
-        lifted = q_li[:, c].astype(F32) * mixed[:, c]
-        inner = inner + jnp.sum(lifted * value_total * gain[:, c], axis=1)
-    inner = lax.psum(inner, "ch")[:, None]
-    weighted = jnp.concatenate(value_totals, axis=1) * gain
+    values = (q_li.astype(F32) * mixed * inv_rms * gain).astype(BF16)
+    attended, d_q_att, d_k_att, value_total = attend(
+        start, q_att, cotangent, key_list, values, lax.axis_size("ctx")
+    )
+    weighted = value_total * gain
+    inner = lax.psum(jnp.sum(q_li.astype(F32) * mixed * weighted, axis=1), "ch")[:, None]
     query = q_li.astype(F32)
     lifted_grad = inv_rms * weighted - query * mixed * (inv_rms**3) * inner / D
     d_q_li = (lifted_grad * mixed).astype(BF16)

time: 501 us -> 450 us (0.90)
  Pallas kernels: 108 us -> 246 us
  waiting for transfers between devices: 228 us -> 137 us
  starting transfers between devices: 103 us -> 12.4 us
  other arithmetic: 26 us -> 20.7 us
    pallas_call x4 -> x1, Pallas kernels: 58.8 us -> 197 us  [attend(): pl.pallas_call(functools.partial(attention, tokens, heads, slabs, span),...]
    ppermute x34 -> x4, waiting for transfers between devices: 198 us -> 95 us  [shifted(): lax.ppermute(value, axis, [(source, source + steps) for source in range(i...]
    ppermute x34 -> x4, starting transfers between devices: 103 us -> 12.3 us  [shifted(): lax.ppermute(value, axis, [(source, source + steps) for source in range(i...]
    all_gather x2, waiting for transfers between devices: 29.1 us -> 41.7 us  [carried_state(): collected = lax.all_gather(local_state[None], 'ctx', axis=0, tiled=True)]
  transfers between devices with their start and end apart: 36 -> 6, of which waited for: 21 -> 3; matrix products, arithmetic and copies ran while one was open for 5% -> 2% of each run, Pallas kernels for 14% -> 4%
where the time goes in v2:
time: 450 us; the launch traced here: 447 us
  Pallas kernels  246 us (55%)
  waiting for transfers between devices  137 us (30%)
  other arithmetic  20.7 us (5%)
  between operations  14.2 us (3%)
  starting transfers between devices  12.4 us (3%)
  blocking collectives  11.6 us (3%)
  local copies, waits for them, and re-layouts  5.4 us (1%)
    pallas_call x1, Pallas kernels, attend(): pl.pallas_call(functools.partial(attention, tokens, heads, slabs, span),...  197 us
    ppermute x4, waiting for transfers between devices, shifted(): lax.ppermute(value, axis, [(source, source + steps) for source in range(i...  95 us
    pallas_call x4, Pallas kernels, conv_call(): pl.pallas_call(body, grid=(channels // width,), in_specs=[specs[kind] for...  49.4 us
    all_gather x2, waiting for transfers between devices, carried_state(): collected = lax.all_gather(local_state[None], 'ctx', axis=0, tiled=True)  41.7 us
    ppermute x4, starting transfers between devices, shifted(): lax.ppermute(value, axis, [(source, source + steps) for source in range(i...  12.3 us
  transfers between devices with their start and end apart: 6, of which 3 were waited for; matrix products, arithmetic and copies ran while one was open for 2% of the time, Pallas kernels for 4%

profile of v2, /device:TPU:8, one launch (start us, length us, event | category | flops | bytes accessed | tf_op | source)
XLA Modules:
  0.0 447.2 jit_solution(5654244669338450080)
XLA Ops:
  7.2 0.0 all-gather.5.cloned.1.call-start
  7.2 1.1 negate_bitcast_fusion
  8.3 0.7 copy.36
  9.0 8.3 %forward_ends.1 = f32[2,16,8,128]{3,2,1,0:T(8,128)} custom-call(bf16[512,2048]{1,0:T(8,128)(2,1)} %k_ref.5, bf16[512,2048]{1,0:T(8,128)(2,1)} %v_ref.5, f32[2,16,8,128]{3,2,1,0:T(8,128)} %bitcast.23), custom_call_target="tpu_custom_call" | custom-call | flops 33554432 | bytes 12582912 | tf_op jit(solution)/shard_map/forward_ends/pallas_call | solution.py:131
  17.3 0.0 all-gather.5.cloned.1.call-update
  17.3 0.0 all-gather.7.cloned.1.call-start
  17.3 3.5 collective-permute-start.2
  20.8 3.4 collective-permute-start.3
  24.3 3.5 collective-permute-start
  27.8 1.9 collective-permute-start.1
  29.8 0.7 copy.35
  30.5 49.1 %collective-permute-done = s32[512]{0:T(512)S(1)} collective-permute-done((s32[512]{0:T(512)S(1)}, s32[512]{0:T(512)S(1)}, u32[]{:S(2)}, u32[]{:S(2)}) %collective-permute-start) | collective-permute-done | bytes 2080 | tf_op jit(solution)/shard_map/ppermute | solution.py:29
  79.6 45.9 %collective-permute-done.1 = s32[512]{0:T(512)S(1)} collective-permute-done((s32[512]{0:T(512)S(1)}, s32[512]{0:T(512)S(1)}, u32[]{:S(2)}, u32[]{:S(2)}) %collective-permute-start.1) | collective-permute-done | bytes 2080 | tf_op jit(solution)/shard_map/ppermute | solution.py:29
  125.5 1.0 convert_reduce_fusion
  126.5 2.2 multiply_reduce_fusion.2.state_ref
  128.6 15.9 %forward_mix.1 = (f32[512,2048]{1,0:T(8,128)}, f32[512,128]{1,0:T(8,128)}) custom-call(bf16[512,2048]{1,0:T(8,128)(2,1)} %k_ref.5, bf16[512,2048]{1,0:T(8,128)(2,1)} %v_ref.5, bf16[512,2048]{1,0:T(8,128)(2,1)} %q_ref.2, f32[2,16,8,128]{3,2,1,0:T(8,128)} %bitcast.24, f32[2,16,8,128]{3,2,1,0:T(8,128)} %bitcast.27, ...), custom_call_target="tpu_custom_call" | custom-call | flops 67108864 | bytes 12582912 | tf_op jit(solution)/shard_map/forward_mix/pallas_call | solution.py:131
  144.6 1.1 reduce_sum.47
  145.7 5.8 %psum.14 = f32[512]{0:T(512)S(1)} all-reduce(f32[512]{0:T(512)S(1)} %reduce_sum.47), channel_id=1, replica_groups=mesh['ctx'=8,'ch'=4] {'ch'}, use_global_device_ids=true, to_apply=%region_3.4 | all-reduce | flops 512 | bytes 4096 | tf_op jit(solution)/shard_map/psum | solution.py:389
  151.4 4.1 multiply_convert_fusion.1.refs_3_
  155.6 0.0 collective-permute-done.2.refs_0_
  155.6 196.7 %attention.1 = (bf16[512,2048]{1,0:T(8,128)(2,1)}, bf16[512,2048]{1,0:T(8,128)(2,1)}, bf16[512,2048]{1,0:T(8,128)(2,1)}, f32[512,2048]{1,0:T(8,128)}) custom-call(s32[1,512]{1,0:T(1,128)} %bitcast.35, bf16[512,2048]{1,0:T(8,128)(2,1)} %q_ref.3, bf16[512,2048]{1,0:T(8,128)(2,1)} %g_ref.1, bf16[512,2048]{1,0:T(8,128)(2,1)} %collective-permute-done.2.refs_0_, ...), custom_call_target="tpu_custom_call" | custom-call | flops 19327352832 | bytes 33554432 | tf_op jit(solution)/shard_map/attention/pallas_call | solution.py:325
  352.4 2.9 multiply_reduce_fusion
  355.3 5.8 %psum.15 = f32[512]{0:T(512)S(1)} all-reduce(f32[512]{0:T(512)S(1)} %multiply_reduce_fusion), channel_id=1, replica_groups=mesh['ctx'=8,'ch'=4] {'ch'}, use_global_device_ids=true, to_apply=%region_5.6 | all-reduce | flops 512 | bytes 4096 | tf_op jit(solution)/shard_map/psum | solution.py:397
  361.1 6.1 %fusion = (bf16[512,2048]{1,0:T(8,128)(2,1)}, bf16[512,2048]{1,0:T(8,128)(2,1)}) fusion(bf16[512,2048]{1,0:T(8,128)(2,1)S(1)} %copy-done.1, f32[512]{0:T(512)S(1)} %psum.15, f32[512,2048]{1,0:T(8,128)} %get-tuple-element.19, f32[512,2048]{1,0:T(8,128)} %get-tuple-element.14, f32[512]{0:T(512)S(1)} %get-tuple-element.27, f32[2048]{0:T(1024)S(1)} %copy-done.5, ...), kind=kLoop, calls=%fused_computation.2 | loop fusion | flops 12582912 | bytes 14694400 | tf_op jit(solution)/shard_map/convert_element_type | solution.py:401
  367.3 7.8 %backward_ends.1 = f32[2,16,8,128]{3,2,1,0:T(8,128)} custom-call(bf16[512,2048]{1,0:T(8,128)(2,1)} %get-tuple-element.22.g_ref, f32[2,16,8,128]{3,2,1,0:T(8,128)} %bitcast.25), custom_call_target="tpu_custom_call" | custom-call | flops 33554432 | bytes 12582912 | tf_op jit(solution)/shard_map/backward_ends/pallas_call | solution.py:131
  375.1 0.0 all-gather.7.cloned.1.call-update
  375.1 41.7 %all-gather.7.cloned.1.call-done = f32[16,16,8,128]{3,2,1,0:T(8,128)} async-done(((f32[2,16,8,128]{3,2,1,0:T(8,128)}), f32[16,16,8,128]{3,2,1,0:T(8,128)}) %all-gather.7.cloned.1.call-update) | async-done | bytes 1048592 | tf_op jit(solution)/shard_map/all_gather | solution.py:148
  416.8 2.2 multiply_reduce_fusion.1.state_ref
  419.0 17.4 %backward_mix.1 = (bf16[512,2048]{1,0:T(8,128)(2,1)}, bf16[512,2048]{1,0:T(8,128)(2,1)}) custom-call(bf16[512,2048]{1,0:T(8,128)(2,1)} %get-tuple-element.22.g_ref, bf16[512,2048]{1,0:T(8,128)(2,1)} %k_ref.5, bf16[512,2048]{1,0:T(8,128)(2,1)} %v_ref.5, f32[2,16,8,128]{3,2,1,0:T(8,128)} %bitcast.26, f32[2,16,8,128]{3,2,1,0:T(8,128)} %bitcast.28, ...), custom_call_target="tpu_custom_call" | custom-call | flops 67108864 | bytes 12582912 | tf_op jit(solution)/shard_map/backward_mix/pallas_call | solution.py:131
  436.4 1.3 copy.40
  437.7 1.3 copy.41
  439.0 1.3 copy.42
  (26 shorter events, 0.2 us)
Async XLA Ops:
  7.2 17.1 %copy-start.6 = (s32[512]{0:T(512)S(1)}, s32[512]{0:T(512)}, u32[]{:S(2)}) copy-start(s32[512]{0:T(512)} %param.16) | copy-start | bytes 6148
  7.2 119.3 %all-gather.5.cloned.1.call-start = ((), (), s32[]{:S(2)}) async-start(), calls=%async_computation | async-start | bytes 1179648 | tf_op jit(solution)/shard_map/all_gather | solution.py:148
  17.3 399.5 %all-gather.7.cloned.1.call-start = ((), (), s32[]{:S(2)}) async-start(), calls=%async_computation.1 | async-start | bytes 1179648 | tf_op jit(solution)/shard_map/all_gather | solution.py:148
  17.3 138.3 %collective-permute-start.2 = (bf16[512,2048]{1,0:T(8,128)(2,1)}, bf16[512,2048]{1,0:T(8,128)(2,1)}, u32[]{:S(2)}, u32[]{:S(2)}) collective-permute-start(bf16[512,2048]{1,0:T(8,128)(2,1)} %refs_2_.1), channel_id=1, source_target_pairs={{0,8},{4,12},{8,16},{12,20},{16,24},{20,28},{1,9},{5,13},{9,17},{1... | collective-permute-start | bytes 6291464 | tf_op jit(solution)/shard_map/ppermute | solution.py:29
  20.8 134.8 %collective-permute-start.3 = (bf16[512,2048]{1,0:T(8,128)(2,1)}, bf16[512,2048]{1,0:T(8,128)(2,1)}, u32[]{:S(2)}, u32[]{:S(2)}) collective-permute-start(bf16[512,2048]{1,0:T(8,128)(2,1)} %refs_2_.1), channel_id=1, source_target_pairs={{0,4},{4,8},{8,12},{12,16},{16,20},{20,24},{24,28},{1,5},{5,9},{9,... | collective-permute-start | bytes 6291464 | tf_op jit(solution)/shard_map/ppermute | solution.py:29
  24.3 55.3 %collective-permute-start = (s32[512]{0:T(512)S(1)}, s32[512]{0:T(512)S(1)}, u32[]{:S(2)}, u32[]{:S(2)}) collective-permute-start(s32[512]{0:T(512)S(1)} %broadcast_add_fusion), channel_id=1, source_target_pairs={{0,8},{4,12},{8,16},{12,20},{16,24},{20,28},{1,9},{5,13},{9,17},{1... | collective-permute-start | bytes 6152 | tf_op jit(solution)/shard_map/ppermute | solution.py:29
  27.8 97.7 %collective-permute-start.1 = (s32[512]{0:T(512)S(1)}, s32[512]{0:T(512)S(1)}, u32[]{:S(2)}, u32[]{:S(2)}) collective-permute-start(s32[512]{0:T(512)S(1)} %broadcast_add_fusion), channel_id=1, source_target_pairs={{0,4},{4,8},{8,12},{12,16},{16,20},{20,24},{24,28},{1,5},{5,9},{9,... | collective-permute-start | bytes 6152 | tf_op jit(solution)/shard_map/ppermute | solution.py:29
  30.5 121.0 %copy-start.1 = (bf16[512,2048]{1,0:T(8,128)(2,1)S(1)}, bf16[512,2048]{1,0:T(8,128)(2,1)}, u32[]{:S(2)}) copy-start(bf16[512,2048]{1,0:T(8,128)(2,1)} %q_ref.2) | copy-start | bytes 6291460
  30.5 121.0 %copy-start.5 = (f32[2048]{0:T(1024)S(1)}, f32[2048]{0:T(1024)}, u32[]{:S(2)}) copy-start(f32[2048]{0:T(1024)} %param.19) | copy-start | bytes 24580
  155.6 196.8 %copy-start = (f32[512,2048]{1,0:T(8,128)S(1)}, f32[512,2048]{1,0:T(8,128)}, u32[]{:S(2)}) copy-start(f32[512,2048]{1,0:T(8,128)} %get-tuple-element.14) | copy-start | bytes 12582916
  375.1 61.3 %copy-start.4 = (bf16[512,2048]{1,0:T(8,128)(2,1)S(1)}, bf16[512,2048]{1,0:T(8,128)(2,1)}, u32[]{:S(2)}) copy-start(bf16[512,2048]{1,0:T(8,128)(2,1)} %get-tuple-element.35) | copy-start | bytes 6291460
  419.0 18.7 %copy-start.3 = (bf16[512,2048]{1,0:T(8,128)(2,1)S(1)}, bf16[512,2048]{1,0:T(8,128)(2,1)}, u32[]{:S(2)}) copy-start(bf16[512,2048]{1,0:T(8,128)(2,1)} %get-tuple-element.36) | copy-start | bytes 6291460
  436.4 2.7 copy-start.2
Sparse Core Ops, SparseCore 0:
  17.4 45.8 all-gather.4
  375.2 41.5 all-gather.6

commit v3 on v2

--- a/solution.py
+++ b/solution.py
@@ -160,10 +160,9 @@
 
 
 def attention(tokens, heads, slabs, span, start_ref, q_ref, g_ref, *refs):
-    key_refs, refs = refs[: span + 1], refs[span + 1 :]
-    own_values, out_ref, dq_ref, dk_ref, dv_ref = refs[:5]
-    bias, keys, values, dkeys, dvalues, far_values, sent, landed, own = refs[5:14]
-    value_send, value_recv, grad_send, grad_recv = refs[14:]
+    own_keys, own_values, out_ref, dq_ref, dk_ref, dv_ref = refs[:6]
+    bias, keys, values, dkeys, dvalues, far, sent, landed, own = refs[6:15]
+    far_send, far_recv, grad_send, grad_recv = refs[15:]
     total = (span + 1) * tokens
     base = span * tokens
     scale = HEAD_DIM ** (-0.5)
@@ -172,12 +171,12 @@
     me = lax.axis_index("ctx")
     distances = range(span, 0, -1)
 
-    def value_copy(d, h):
+    def far_copy(kind, d, h):
         return pltpu.make_async_remote_copy(
-            src_ref=own_values.at[:, pl.ds(pl.multiple_of(h * HEAD_DIM, HEAD_DIM), HEAD_DIM)],
-            dst_ref=far_values.at[d - 1, h],
-            send_sem=value_send.at[d - 1, h],
-            recv_sem=value_recv.at[d - 1, h],
+            src_ref=(own_keys, own_values)[kind].at[:, pl.ds(pl.multiple_of(h * HEAD_DIM, HEAD_DIM), HEAD_DIM)],
+            dst_ref=far.at[kind, d - 1, h],
+            send_sem=far_send.at[kind, d - 1, h],
+            recv_sem=far_recv.at[kind, d - 1, h],
             device_id={"ctx": lax.rem(me + d, slabs)},
             device_id_type=pl.DeviceIdType.MESH,
         )
@@ -220,7 +219,11 @@
         @pl.loop(0, heads)
         def _(h):
             for d in distances:
-                pl.when(me + d < slabs)(lambda d=d: value_copy(d, h).start())
+
+                @pl.when(me + d < slabs)
+                def _(d=d):
+                    far_copy(0, d, h).start()
+                    far_copy(1, d, h).start()
 
         for low in range(0, total, tokens):
             place = low + lax.broadcasted_iota(jnp.int32, (tokens, tokens), 0)
@@ -236,16 +239,19 @@
 
             @pl.when(me >= d)
             def _(d=d, slab=slab):
-                value_copy(d, h).wait_recv()
-                values[slab, :] = far_values[d - 1, h]
+                far_copy(0, d, h).wait_recv()
+                far_copy(1, d, h).wait_recv()
+                keys[slab, :] = far[0, d - 1, h]
+                values[slab, :] = far[1, d - 1, h]
 
             @pl.when(me < d)
             def _(d=d, slab=slab):
+                keys[slab, :] = jnp.zeros((tokens, HEAD_DIM), BF16)
                 values[slab, :] = jnp.zeros((tokens, HEAD_DIM), BF16)
 
-        values[base:, :] = own_values[:, pl.ds(pl.multiple_of(h * HEAD_DIM, HEAD_DIM), HEAD_DIM)]
-        for j in range(span + 1):
-            keys[j * tokens : (j + 1) * tokens, :] = key_refs[j][...]
+        head = pl.ds(pl.multiple_of(h * HEAD_DIM, HEAD_DIM), HEAD_DIM)
+        keys[base:, :] = own_keys[:, head]
+        values[base:, :] = own_values[:, head]
         dkeys[...] = jnp.zeros_like(dkeys)
         dvalues[...] = jnp.zeros_like(dvalues)
         size = QUERY_BLOCK
@@ -293,7 +299,8 @@
 
             @pl.when(me + d < slabs)
             def _(d=d):
-                value_copy(d, h).wait_send()
+                far_copy(0, d, h).wait_send()
+                far_copy(1, d, h).wait_send()
                 grad_copy(0, d, h).wait_recv()
                 grad_copy(1, d, h).wait_recv()
 
@@ -314,9 +321,9 @@
         dv_ref[...] = sums[1]
 
 
-def attend(start, q_att, cotangent, key_list, values, slabs):
+def attend(start, q_att, cotangent, k_att, values, slabs):
     tokens, channels = q_att.shape
-    span = len(key_list) - 1
+    span = SPAN
     heads = channels // HEAD_DIM
     first = pl.BlockSpec((tokens, HEAD_DIM), lambda h: (0, jnp.minimum(h, heads - 1)))
     second = pl.BlockSpec((tokens, HEAD_DIM), lambda h: (0, jnp.maximum(h - heads, 0)))
@@ -326,8 +333,8 @@
         functools.partial(attention, tokens, heads, slabs, span),
         grid=(2 * heads,),
         in_specs=[pl.BlockSpec((1, tokens), lambda h: (0, 0))]
-        + [first] * (3 + span)
-        + [pl.BlockSpec(memory_space=pltpu.VMEM)],
+        + [first] * 2
+        + [pl.BlockSpec(memory_space=pltpu.VMEM)] * 2,
         out_specs=[first, first, second, second],
         out_shape=[low, low, low, jax.ShapeDtypeStruct((tokens, channels), F32)],
         scratch_shapes=[
@@ -336,12 +343,12 @@
             pltpu.VMEM((total, HEAD_DIM), BF16),
             pltpu.VMEM((total, HEAD_DIM), F32),
             pltpu.VMEM((total, HEAD_DIM), F32),
-            pltpu.VMEM((span, heads, tokens, HEAD_DIM), BF16),
+            pltpu.VMEM((2, span, heads, tokens, HEAD_DIM), BF16),
             pltpu.VMEM((2, span, heads, tokens, HEAD_DIM), BF16),
             pltpu.VMEM((2, span, heads, tokens, HEAD_DIM), BF16),
             pltpu.VMEM((2, heads, tokens, HEAD_DIM), BF16),
-            pltpu.SemaphoreType.DMA((span, heads)),
-            pltpu.SemaphoreType.DMA((span, heads)),
+            pltpu.SemaphoreType.DMA((2, span, heads)),
+            pltpu.SemaphoreType.DMA((2, span, heads)),
             pltpu.SemaphoreType.DMA((2, span, heads)),
             pltpu.SemaphoreType.DMA((2, span, heads)),
         ],
@@ -352,7 +359,7 @@
             transcendentals=heads * tokens * total,
         ),
         name="attention",
-    )(start, q_att, cotangent, *key_list, values)
+    )(start, q_att, cotangent, k_att, values)
 
 
 def local(q_li, k_li, v_li, q_att, k_att, cotangent, record_ids, decay_rate, residue, norm_gain):
@@ -374,7 +381,6 @@
     all_marks = jnp.concatenate(all_marks)
     start = jnp.sum((all_marks[:, None] < marks[None, :]).astype(jnp.int32), axis=0)
     start = start[None, :]
-    key_list = [shifted(k_att, "ctx", d) for d in range(SPAN, 0, -1)] + [k_att]
 
     (ends,) = call(
         forward_ends, "forward_ends", in_kinds=("wide", "wide", "mode"), out_kinds=(("mode", F32),),
@@ -391,7 +397,7 @@
 
     values = (q_li.astype(F32) * mixed * inv_rms * gain).astype(BF16)
     attended, d_q_att, d_k_att, value_total = attend(
-        start, q_att, cotangent, key_list, values, lax.axis_size("ctx")
+        start, q_att, cotangent, k_att, values, lax.axis_size("ctx")
     )
     weighted = value_total * gain
     inner = lax.psum(jnp.sum(q_li.astype(F32) * mixed * weighted, axis=1), "ch")[:, None]

time: 450 us -> 388 us (0.86)
  waiting for transfers between devices: 137 us -> 73.1 us
  Pallas kernels: 246 us -> 253 us
  starting transfers between devices: 12.4 us -> 6.99 us
    ppermute x4 -> x2, waiting for transfers between devices: 95 us -> 1.19 us  [shifted(): lax.ppermute(value, axis, [(source, source + steps) for source in range(i...]
    all_gather x2, waiting for transfers between devices: 41.7 us -> 71.9 us  [carried_state(): collected = lax.all_gather(local_state[None], 'ctx', axis=0, tiled=True)]
    pallas_call x1, Pallas kernels: 197 us -> 203 us  [attend(): pl.pallas_call(functools.partial(attention, tokens, heads, slabs, span),...]
    ppermute x4 -> x2, starting transfers between devices: 12.3 us -> 6.91 us  [shifted(): lax.ppermute(value, axis, [(source, source + steps) for source in range(i...]
  transfers between devices with their start and end apart: 6 -> 4, of which waited for: 3 -> 3; matrix products, arithmetic and copies ran while one was open for 2% -> 0% of each run, Pallas kernels for 4% -> 0%
where the time goes in v3:
time: 388 us; the launch traced here: 385 us
  Pallas kernels  253 us (65%)
  waiting for transfers between devices  73.1 us (19%)
  other arithmetic  20.7 us (5%)
  between operations  14.2 us (4%)
  blocking collectives  11.7 us (3%)
  starting transfers between devices  6.99 us (2%)
  local copies, waits for them, and re-layouts  5.4 us (1%)
    pallas_call x1, Pallas kernels, attend(): pl.pallas_call(functools.partial(attention, tokens, heads, slabs, span),...  203 us
    all_gather x2, waiting for transfers between devices, carried_state(): collected = lax.all_gather(local_state[None], 'ctx', axis=0, tiled=True)  71.9 us
    pallas_call x4, Pallas kernels, conv_call(): pl.pallas_call(body, grid=(channels // width,), in_specs=[specs[kind] for...  49.4 us
  transfers between devices with their start and end apart: 4, of which 3 were waited for; matrix products, arithmetic and copies ran while one was open for 0% of the time, Pallas kernels for 0%

profile of v3, /device:TPU:8, one launch (start us, length us, event | category | flops | bytes accessed | tf_op | source)
XLA Modules:
  0.0 384.8 jit_solution(8035139783358116890)
XLA Ops:
  7.2 0.0 all-gather.5.cloned.1.call-start
  7.2 1.1 negate_bitcast_fusion
  8.3 0.7 copy.36
  9.0 8.3 %forward_ends.1 = f32[2,16,8,128]{3,2,1,0:T(8,128)} custom-call(bf16[512,2048]{1,0:T(8,128)(2,1)} %k_ref.5, bf16[512,2048]{1,0:T(8,128)(2,1)} %v_ref.5, f32[2,16,8,128]{3,2,1,0:T(8,128)} %bitcast.23), custom_call_target="tpu_custom_call" | custom-call | flops 33554432 | bytes 12582912 | tf_op jit(solution)/shard_map/forward_ends/pallas_call | solution.py:131
  17.3 0.0 all-gather.5.cloned.1.call-update
  17.3 0.0 all-gather.7.cloned.1.call-start
  17.3 3.4 collective-permute-start.1
  20.8 3.5 collective-permute-start
  24.3 0.7 copy.35
  25.0 0.0 copy-start.1
  25.0 0.0 copy-start.5
  25.1 0.0 collective-permute-done.1
  25.1 1.2 collective-permute-done
  26.3 1.0 convert_reduce_fusion
  27.2 30.6 %all-gather.5.cloned.1.call-done = f32[16,16,8,128]{3,2,1,0:T(8,128)} async-done(((f32[2,16,8,128]{3,2,1,0:T(8,128)}), f32[16,16,8,128]{3,2,1,0:T(8,128)}) %all-gather.5.cloned.1.call-update) | async-done | bytes 1048592 | tf_op jit(solution)/shard_map/all_gather | solution.py:148
  57.8 2.2 multiply_reduce_fusion.2.state_ref
  60.0 16.0 %forward_mix.1 = (f32[512,2048]{1,0:T(8,128)}, f32[512,128]{1,0:T(8,128)}) custom-call(bf16[512,2048]{1,0:T(8,128)(2,1)} %k_ref.5, bf16[512,2048]{1,0:T(8,128)(2,1)} %v_ref.5, bf16[512,2048]{1,0:T(8,128)(2,1)} %q_ref.2, f32[2,16,8,128]{3,2,1,0:T(8,128)} %bitcast.24, f32[2,16,8,128]{3,2,1,0:T(8,128)} %bitcast.27, ...), custom_call_target="tpu_custom_call" | custom-call | flops 67108864 | bytes 12582912 | tf_op jit(solution)/shard_map/forward_mix/pallas_call | solution.py:131
  75.9 1.1 reduce_sum.47
  77.0 5.9 %psum.14 = f32[512]{0:T(512)S(1)} all-reduce(f32[512]{0:T(512)S(1)} %reduce_sum.47), channel_id=1, replica_groups=mesh['ctx'=8,'ch'=4] {'ch'}, use_global_device_ids=true, to_apply=%region_3.4 | all-reduce | flops 512 | bytes 4096 | tf_op jit(solution)/shard_map/psum | solution.py:395
  82.9 4.1 %multiply_convert_fusion.1.refs_1_ = bf16[512,2048]{1,0:T(8,128)(2,1)} fusion(f32[512,2048]{1,0:T(8,128)} %get-tuple-element.14, bf16[512,2048]{1,0:T(8,128)(2,1)S(1)} %copy-done.1, f32[2048]{0:T(1024)S(1)} %copy-done.5, f32[512]{0:T(512)S(1)} %get-tuple-element.28), kind=kLoop, calls=%fused_computation.6 | loop fusion | flops 5242880 | bytes 8398848 | tf_op jit(solution)/shard_map/convert_element_type | solution.py:398
  87.1 203.2 %attention.1 = (bf16[512,2048]{1,0:T(8,128)(2,1)}, bf16[512,2048]{1,0:T(8,128)(2,1)}, bf16[512,2048]{1,0:T(8,128)(2,1)}, f32[512,2048]{1,0:T(8,128)}) custom-call(s32[1,512]{1,0:T(1,128)} %bitcast.35, bf16[512,2048]{1,0:T(8,128)(2,1)} %q_ref.3, bf16[512,2048]{1,0:T(8,128)(2,1)} %g_ref.1, bf16[512,2048]{1,0:T(8,128)(2,1)} %refs_0_.1, ...), custom_call_target="tpu_custom_call" | custom-call | flops 19327352832 | bytes 33554432 | tf_op jit(solution)/shard_map/attention/pallas_call | solution.py:332
  290.3 2.9 multiply_reduce_fusion
  293.2 5.8 %psum.15 = f32[512]{0:T(512)S(1)} all-reduce(f32[512]{0:T(512)S(1)} %multiply_reduce_fusion), channel_id=1, replica_groups=mesh['ctx'=8,'ch'=4] {'ch'}, use_global_device_ids=true, to_apply=%region_5.6 | all-reduce | flops 512 | bytes 4096 | tf_op jit(solution)/shard_map/psum | solution.py:403
  299.1 6.1 %fusion = (bf16[512,2048]{1,0:T(8,128)(2,1)}, bf16[512,2048]{1,0:T(8,128)(2,1)}) fusion(bf16[512,2048]{1,0:T(8,128)(2,1)S(1)} %copy-done.1, f32[512]{0:T(512)S(1)} %psum.15, f32[512,2048]{1,0:T(8,128)} %get-tuple-element.19, f32[512,2048]{1,0:T(8,128)} %get-tuple-element.14, f32[512]{0:T(512)S(1)} %get-tuple-element.27, f32[2048]{0:T(1024)S(1)} %copy-done.5, ...), kind=kLoop, calls=%fused_computation.2 | loop fusion | flops 12582912 | bytes 14694400 | tf_op jit(solution)/shard_map/convert_element_type | solution.py:407
  305.2 7.8 %backward_ends.1 = f32[2,16,8,128]{3,2,1,0:T(8,128)} custom-call(bf16[512,2048]{1,0:T(8,128)(2,1)} %get-tuple-element.22.g_ref, f32[2,16,8,128]{3,2,1,0:T(8,128)} %bitcast.25), custom_call_target="tpu_custom_call" | custom-call | flops 33554432 | bytes 12582912 | tf_op jit(solution)/shard_map/backward_ends/pallas_call | solution.py:131
  313.0 0.0 all-gather.7.cloned.1.call-update
  313.1 41.3 %all-gather.7.cloned.1.call-done = f32[16,16,8,128]{3,2,1,0:T(8,128)} async-done(((f32[2,16,8,128]{3,2,1,0:T(8,128)}), f32[16,16,8,128]{3,2,1,0:T(8,128)}) %all-gather.7.cloned.1.call-update) | async-done | bytes 1048592 | tf_op jit(solution)/shard_map/all_gather | solution.py:148
  354.4 2.2 multiply_reduce_fusion.1.state_ref
  356.5 17.4 %backward_mix.1 = (bf16[512,2048]{1,0:T(8,128)(2,1)}, bf16[512,2048]{1,0:T(8,128)(2,1)}) custom-call(bf16[512,2048]{1,0:T(8,128)(2,1)} %get-tuple-element.22.g_ref, bf16[512,2048]{1,0:T(8,128)(2,1)} %k_ref.5, bf16[512,2048]{1,0:T(8,128)(2,1)} %v_ref.5, f32[2,16,8,128]{3,2,1,0:T(8,128)} %bitcast.26, f32[2,16,8,128]{3,2,1,0:T(8,128)} %bitcast.28, ...), custom_call_target="tpu_custom_call" | custom-call | flops 67108864 | bytes 12582912 | tf_op jit(solution)/shard_map/backward_mix/pallas_call | solution.py:131
  373.9 1.3 copy.40
  375.3 1.3 copy.41
  376.6 1.3 copy.42
  (22 shorter events, 0.2 us)
Async XLA Ops:
  7.2 10.2 %copy-start.6 = (s32[512]{0:T(512)S(1)}, s32[512]{0:T(512)}, u32[]{:S(2)}) copy-start(s32[512]{0:T(512)} %param.16) | copy-start | bytes 6148
  7.2 50.6 %all-gather.5.cloned.1.call-start = ((), (), s32[]{:S(2)}) async-start(), calls=%async_computation | async-start | bytes 1179648 | tf_op jit(solution)/shard_map/all_gather | solution.py:148
  17.3 337.1 %all-gather.7.cloned.1.call-start = ((), (), s32[]{:S(2)}) async-start(), calls=%async_computation.1 | async-start | bytes 1179648 | tf_op jit(solution)/shard_map/all_gather | solution.py:148
  17.3 7.7 %collective-permute-start.1 = (s32[512]{0:T(512)S(1)}, s32[512]{0:T(512)S(1)}, u32[]{:S(2)}, u32[]{:S(2)}) collective-permute-start(s32[512]{0:T(512)S(1)} %broadcast_add_fusion), channel_id=1, source_target_pairs={{0,4},{4,8},{8,12},{12,16},{16,20},{20,24},{24,28},{1,5},{5,9},{9,... | collective-permute-start | bytes 6152 | tf_op jit(solution)/shard_map/ppermute | solution.py:29
  20.8 5.5 %collective-permute-start = (s32[512]{0:T(512)S(1)}, s32[512]{0:T(512)S(1)}, u32[]{:S(2)}, u32[]{:S(2)}) collective-permute-start(s32[512]{0:T(512)S(1)} %broadcast_add_fusion), channel_id=1, source_target_pairs={{0,8},{4,12},{8,16},{12,20},{16,24},{20,28},{1,9},{5,13},{9,17},{1... | collective-permute-start | bytes 6152 | tf_op jit(solution)/shard_map/ppermute | solution.py:29
  25.0 57.9 %copy-start.1 = (bf16[512,2048]{1,0:T(8,128)(2,1)S(1)}, bf16[512,2048]{1,0:T(8,128)(2,1)}, u32[]{:S(2)}) copy-start(bf16[512,2048]{1,0:T(8,128)(2,1)} %q_ref.2) | copy-start | bytes 6291460
  25.0 57.9 %copy-start.5 = (f32[2048]{0:T(1024)S(1)}, f32[2048]{0:T(1024)}, u32[]{:S(2)}) copy-start(f32[2048]{0:T(1024)} %param.19) | copy-start | bytes 24580
  87.1 203.2 %copy-start = (f32[512,2048]{1,0:T(8,128)S(1)}, f32[512,2048]{1,0:T(8,128)}, u32[]{:S(2)}) copy-start(f32[512,2048]{1,0:T(8,128)} %get-tuple-element.14) | copy-start | bytes 12582916
  313.0 60.9 %copy-start.4 = (bf16[512,2048]{1,0:T(8,128)(2,1)S(1)}, bf16[512,2048]{1,0:T(8,128)(2,1)}, u32[]{:S(2)}) copy-start(bf16[512,2048]{1,0:T(8,128)(2,1)} %get-tuple-element.35) | copy-start | bytes 6291460
  356.5 18.7 %copy-start.3 = (bf16[512,2048]{1,0:T(8,128)(2,1)S(1)}, bf16[512,2048]{1,0:T(8,128)(2,1)}, u32[]{:S(2)}) copy-start(bf16[512,2048]{1,0:T(8,128)(2,1)} %get-tuple-element.36) | copy-start | bytes 6291460
  373.9 2.7 copy-start.2
Sparse Core Ops, SparseCore 0:
  17.4 40.3 all-gather.4
  313.2 41.1 all-gather.6
